TPU v7x, 512 devices: a whole 4x4x16 slice. The times are simulated.
512 devices in a mesh: row: 32 (over z, core), col: 16 (over x, y).
Axes of the slice: x: 4, y: 4, z: 16, core: 2. Of those that a mesh axis runs over, the one named last changes fastest.
Arguments:
- factor: bfloat16 [128, 16, 8, 128, 128], P('row', 'col'), may hold values from -0.0625 to 0.0625
- index: int32 [128, 16, 8], P('row', 'col'), may hold values from 0 to 15, as said below
- keep: int32 [128, 16, 8, 16], P('row', 'col'), may hold values 0 or 1
- panel: bfloat16 [256, 16, 128, 128], P('col', None, 'row'), may hold values from -6 to 6
Outputs:
- mixed: bfloat16 [128, 16, 128, 128], P('row', 'col')
Inputs may be any that keep to these rules, and one draw needn't show every extreme that they name: For each block row and each index of col, the 8 entries are distinct.
All inputs are finite; a program needn't handle non-finite values. No bound on the sum of `keep` on one device may be relied on, other than what follows from the above.
Results may differ from a plain program's by a relative error of at most 0.001.
Values may be sent and summed in bfloat16 or wider, within the bound.
No kernel may reach another device: no remote copies, remote signals or barrier semaphores. Data moves between devices by JAX's collectives and lax.ppermute only.
A program may use at most 64 MiB of HBM per device.

v0:
```python
import jax
import jax.numpy as jnp
from jax import lax
from jax.sharding import PartitionSpec as P


def per_device(factor, index, keep, panel):
    gathered = lax.all_gather(panel, "row", axis=2, tiled=True)
    slot_rows = index[:, 0, :]
    newton_factor_rows = factor[:, 0]
    keep_rows = keep[:, 0].astype(jnp.bfloat16)

    def group_term(group_id):
        weights = lax.dynamic_index_in_dim(keep_rows, group_id, 2, keepdims=False)
        block_rows = lax.dynamic_index_in_dim(gathered, group_id, 1, keepdims=False)
        chosen_blocks = jnp.take(block_rows, slot_rows, axis=0)
        pattern_masked = newton_factor_rows * weights[:, :, None, None]
        return jnp.einsum(
            "xrun,xrnk->xuk", pattern_masked, chosen_blocks, preferred_element_type=jnp.float32
        )

    incomplete_value = lax.map(group_term, jnp.arange(gathered.shape[1], dtype=jnp.int32))
    output_portion = lax.psum_scatter(incomplete_value, "col", scatter_dimension=0, tiled=True)
    return output_portion.reshape(
        factor.shape[0], 1, output_portion.shape[2], output_portion.shape[3]
    ).astype(jnp.bfloat16)


def solution(mesh):
    return jax.shard_map(
        per_device,
        mesh=mesh,
        in_specs=(
            P("row", "col", None, None, None),
            P("row", "col", None),
            P("row", "col", None, None),
            P("col", None, "row", None),
        ),
        out_specs=P("row", "col", None, None),
        check_vma=False,
    )
```

profile of v0, /device:TPU:2, one launch (start us, length us, event | category | flops | bytes accessed | tf_op | source)
XLA Modules:
  0.0 294.7 jit_solution(9656518237472728155)
XLA Ops:
  6.5 1.7 copy.7
  9.2 84.4 %all-gather.2.cloned.1.call-done = bf16[16,16,128,128]{3,1,0,2:T(8,128)(2,1)} async-done(((bf16[16,16,4,128]{3,1,0,2:T(8,128)(2,1)}), bf16[16,16,128,128]{3,1,0,2:T(8,128)(2,1)}) %all-gather.2.cloned.1.call-update) | async-done | bytes 8388624 | tf_op jit(solution)/shard_map/all_gather | solution.py:8
  93.5 12.0 %copy.8 = bf16[16,16,128,128]{3,2,1,0:T(8,128)(2,1)} copy(bf16[16,16,128,128]{3,1,0,2:T(8,128)(2,1)} %all-gather.2.cloned.1.call-done) | data formatting | bytes 16777216 | tf_op jit(solution)/shard_map/while | solution.py:22
  105.5 91.3 %while.10 = (s32[]{:T(128)}, f32[16,4,128,128]{3,2,1,0:T(8,128)}, s32[16]{0:T(128)S(1)}, bf16[4,8,16]{1,0,2:T(4,128)(2,1)S(1)}, bf16[4,8,128,128]{3,2,1,0:T(8,12...) while((s32[]{:T(128)}, f32[16,4,128,128]{3,2,1,0:T(8,128)}, ...), condition=%wide.region_1.2_spmd, body=%wide.region_0.1_spmd.sunk | while | flops 135267616 | bytes 5510939 | solution.py:22
  108.1 1.1 dynamic-slice_bitcast_fusion.4
  110.0 1.2 fusion.12
  113.8 1.1 dynamic-slice_bitcast_fusion.4
  115.7 1.2 fusion.12
  119.5 1.1 dynamic-slice_bitcast_fusion.4
  121.5 1.2 fusion.12
  125.2 1.1 dynamic-slice_bitcast_fusion.4
  127.2 1.2 fusion.12
  130.9 1.1 dynamic-slice_bitcast_fusion.4
  132.9 1.2 fusion.12
  136.6 1.1 dynamic-slice_bitcast_fusion.4
  138.6 1.2 fusion.12
  142.3 1.1 dynamic-slice_bitcast_fusion.4
  144.3 1.2 fusion.12
  148.0 1.1 dynamic-slice_bitcast_fusion.4
  150.0 1.2 fusion.12
  153.7 1.1 dynamic-slice_bitcast_fusion.4
  155.7 1.2 fusion.12
  161.4 1.2 fusion.12
  165.1 1.1 dynamic-slice_bitcast_fusion.4
  167.1 1.2 fusion.12
  172.8 1.2 fusion.12
  178.5 1.2 fusion.12
  184.2 1.2 fusion.12
  189.9 1.2 fusion.12
  195.6 1.2 fusion.12
  196.8 89.3 %reduce-scatter.4.cloned.1.call-done = f32[1,4,128,128]{3,2,1,0:T(8,128)} async-done(((f32[16,4,128,128]{3,2,1,0:T(8,128)}), f32[1,4,128,128]{3,2,1,0:T(8,128)}) %reduce-scatter.4.cloned.1.call-update) | async-done | bytes 262160
  286.2 1.6 convert_bitcast_fusion
  (130 shorter events, 30.9 us)
Async XLA Ops:
  6.5 87.0 %all-gather.2.cloned.1.call-start = ((), (), s32[]{:S(2)}) async-start(), calls=%async_computation.1 | async-start | bytes 8650752 | tf_op jit(solution)/shard_map/all_gather | solution.py:8
  8.2 277.9 %reduce-scatter.4.cloned.1.call-start = ((), (), s32[]{:S(2)}) async-start(), calls=%async_computation.2 | async-start | bytes 4456448
  9.1 96.4 %copy-start = (s32[4,1,8]{2,1,0:T(1,128)S(1)}, s32[4,1,8]{2,1,0:T(1,128)}, u32[]{:S(2)}) copy-start(s32[4,1,8]{2,1,0:T(1,128)} %param.7) | copy-start | bytes 388
  9.1 96.4 %copy-start.1 = (bf16[4,1,8,128,128]{4,3,2,1,0:T(8,128)(2,1)S(1)}, bf16[4,1,8,128,128]{4,3,2,1,0:T(8,128)(2,1)}, u32[]{:S(2)}) copy-start(bf16[4,1,8,128,128]{4,3,2,1,0:T(8,128)(2,1)} %param.6) | copy-start | bytes 3145732
Sparse Core Ops, SparseCore 0:
  9.5 84.0 all-gather.1
  197.0 89.1 reduce-scatter.3
where the time goes:
time: 296 us; the launch traced here: 295 us
  waiting for transfers between devices  174 us (59%)
  local copies, waits for them, and re-layouts  54.4 us (18%)
  loops' own time  31 us (10%)
  matrix products  19.4 us (7%)
  between operations  13.4 us (5%)
    unnamed x3, waiting for transfers between devices  89.4 us
    all_gather x1, waiting for transfers between devices, per_device(): gathered = lax.all_gather(panel, 'row', axis=2, tiled=True)  84.4 us
    another operation x1, loops' own time, per_device(): lax.map(group_term, jnp.arange(gathered.shape[1], dtype=jnp.int32))  31 us
    dot_general x16, matrix products, group_term(): jnp.einsum('xrun,xrnk->xuk', pattern_masked, chosen_blocks, preferred_ele...  19.4 us
    squeeze x16, local copies, waits for them, and re-layouts, group_term(): block_rows = lax.dynamic_index_in_dim(gathered, group_id, 1, keepdims=False)  17.4 us
    while x1, local copies, waits for them, and re-layouts, per_device(): lax.map(group_term, jnp.arange(gathered.shape[1], dtype=jnp.int32))  12 us
    gather x16, local copies, waits for them, and re-layouts, group_term(): chosen_blocks = jnp.take(block_rows, slot_rows, axis=0)  12 us
    dynamic_slice x16, local copies, waits for them, and re-layouts, per_device(): lax.map(group_term, jnp.arange(gathered.shape[1], dtype=jnp.int32))  9.67 us
  transfers between devices with their start and end apart: 2, of which 2 were waited for; matrix products, arithmetic and copies ran while one was open for 0% of the time, Pallas kernels for 0%

commit v1 on v0

v1 whole, which is shorter than its diff:
```python
import jax
import jax.numpy as jnp
from jax import lax
from jax.experimental import pallas as pl
from jax.experimental.pallas import tpu as pltpu
from jax.sharding import PartitionSpec as P

ROWS = 32
COLS = 16
NBC = 16
SUB = 4
B = 128
DEPTH = NBC * B


def spread_kernel(index_ref, factor_ref, spread_ref):
    i = pl.program_id(0)
    b = lax.broadcasted_iota(jnp.int32, (B, DEPTH), 0)
    col = lax.broadcasted_iota(jnp.int32, (B, DEPTH), 1)
    home = (col // (NBC * SUB)) * SUB + col % SUB
    place = jnp.where(b == home, 1.0, 0.0).astype(jnp.bfloat16)
    block = (lax.broadcasted_iota(jnp.int32, (1, DEPTH), 1) // SUB) % NBC
    total = jnp.zeros((B, DEPTH), jnp.float32)
    for s in range(factor_ref.shape[1]):
        moved = jnp.dot(factor_ref[0, s], place, preferred_element_type=jnp.float32)
        total = jnp.where(block == index_ref[i, s], moved, total)
    spread_ref[0] = total.astype(jnp.bfloat16)


def product_kernel(spread_ref, mask_ref, panel_ref, out_ref):
    rows = panel_ref[:, 0].reshape(DEPTH, B)
    for i in range(spread_ref.shape[0]):
        out_ref[0, i] = jnp.dot(
            spread_ref[i] * mask_ref[0, i : i + 1], rows, preferred_element_type=jnp.float32
        )


def per_device(factor, index, keep, panel):
    n_i = factor.shape[0]
    factor, index, keep = factor[:, 0], index[:, 0], keep[:, 0]
    shard = panel.transpose(1, 0, 2, 3).reshape(COLS, NBC * SUB, B)
    gathered = lax.all_gather(shard, "row", axis=0)

    spread = pl.pallas_call(
        spread_kernel,
        grid=(n_i,),
        in_specs=[
            pl.BlockSpec(memory_space=pltpu.SMEM),
            pl.BlockSpec((1,) + factor.shape[1:], lambda i: (i, 0, 0, 0)),
        ],
        out_specs=pl.BlockSpec((1, B, DEPTH), lambda i: (i, 0, 0)),
        out_shape=jax.ShapeDtypeStruct((n_i, B, DEPTH), jnp.bfloat16),
        compiler_params=pltpu.CompilerParams(vmem_limit_bytes=32 * 2**20),
        cost_estimate=pl.CostEstimate(flops=2 * n_i * 8 * B * B * DEPTH, bytes_accessed=3 * 2**20, transcendentals=0),
    )(index, factor)

    chosen = (index[:, :, None] == jnp.arange(NBC)).astype(jnp.float32)
    kept = jnp.einsum("isk,isg->gik", chosen, keep.astype(jnp.float32))
    mask = jnp.broadcast_to(
        kept.astype(jnp.bfloat16)[:, :, None, :, None], (COLS, n_i, ROWS, NBC, SUB)
    ).reshape(COLS, n_i, DEPTH)

    partial = pl.pallas_call(
        product_kernel,
        grid=(COLS,),
        in_specs=[
            pl.BlockSpec((n_i, B, DEPTH), lambda g: (0, 0, 0)),
            pl.BlockSpec((1, n_i, DEPTH), lambda g: (g, 0, 0)),
            pl.BlockSpec((ROWS, 1, NBC * SUB, B), lambda g: (0, g, 0, 0)),
        ],
        out_specs=pl.BlockSpec((1, n_i, B, B), lambda g: (g, 0, 0, 0)),
        out_shape=jax.ShapeDtypeStruct((COLS, n_i, B, B), jnp.float32),
        compiler_params=pltpu.CompilerParams(vmem_limit_bytes=58 * 2**20),
        cost_estimate=pl.CostEstimate(flops=2 * COLS * n_i * B * B * DEPTH, bytes_accessed=15 * 2**20, transcendentals=0),
    )(spread, mask, gathered)

    parts = lax.all_to_all(partial, "col", 0, 0, tiled=True)
    return jnp.sum(parts, axis=0).astype(jnp.bfloat16)[:, None]


def solution(mesh):
    return jax.shard_map(
        per_device,
        mesh=mesh,
        in_specs=(
            P("row", "col", None, None, None),
            P("row", "col", None),
            P("row", "col", None, None),
            P("col", None, "row", None),
        ),
        out_specs=P("row", "col", None, None),
        check_vma=False,
    )
```

time: 296 us -> 179 us (0.60)
  the two profiles are of different devices: /device:TPU:2 before, /device:TPU:32 now
where the time goes in v1:
time: 179 us; the launch traced here: 178 us
  waiting for transfers between devices  73.9 us (41%)
  blocking collectives  58.1 us (32%)
  Pallas kernels  23 us (13%)
  between operations  13.4 us (7%)
  local copies, waits for them, and re-layouts  5.79 us (3%)
  other arithmetic  3.08 us (2%)
    all_gather x1, waiting for transfers between devices, per_device(): gathered = lax.all_gather(shard, 'row', axis=0)  73.9 us
    all_to_all x1, blocking collectives, per_device(): parts = lax.all_to_all(partial, 'col', 0, 0, tiled=True)  58.1 us
    pallas_call x1, Pallas kernels, per_device(): pl.pallas_call(product_kernel, grid=(COLS,), in_specs=[pl.BlockSpec((n_i,...  17.2 us
    pallas_call x1, Pallas kernels, per_device(): pl.pallas_call(spread_kernel, grid=(n_i,), in_specs=[pl.BlockSpec(memory_...  5.8 us
  transfers between devices with their start and end apart: 1, of which 1 were waited for; matrix products, arithmetic and copies ran while one was open for 2% of the time, Pallas kernels for 3%

profile of v1, /device:TPU:32, one launch (start us, length us, event | category | flops | bytes accessed | tf_op | source)
XLA Modules:
  0.0 178.4 jit_solution(16705615700624807742)
XLA Ops:
  6.5 0.0 copy-start.1
  6.5 0.0 copy-start
  6.5 0.0 all-gather.2.cloned.1.call-start
  6.5 1.9 %copy.9 = bf16[16,16,4,128]{3,2,1,0:T(4,128)(2,1)} copy(bf16[16,16,4,128]{3,2,0,1:T(4,128)(2,1)} %bitcast.18) | data formatting | bytes 524288 | tf_op jit(solution)/shard_map/transpose | solution.py:41
  8.4 0.0 all-gather.2.cloned.1.call-update
  8.5 1.0 fusion
  9.5 1.0 broadcast_in_dim.2
  10.5 1.6 copy.10.mask_ref
  12.0 0.0 copy-done.1
  12.0 0.0 copy-done
  12.0 5.8 %shard_map.46.spread_ref = bf16[4,128,2048]{2,1,0:T(8,128)(2,1)S(1)} custom-call(s32[4,8]{1,0:T(4,128)S(1)} %bitcast.15, bf16[4,8,128,128]{3,2,1,0:T(8,128)(2,1)S(1)} %bitcast.13), custom_call_target="tpu_custom_call" | custom-call | flops 2147483648 | bytes 3145728 | tf_op jit(solution)/shard_map/pallas_call | solution.py:44
  17.9 0.0 copy-start.2
  17.9 1.3 copy-done.2
  19.2 73.9 %all-gather.2.cloned.1.call-done.panel_ref = bf16[32,16,64,128]{3,2,1,0:T(8,128)(2,1)} async-done(((bf16[1,16,64,128]{3,2,1,0:T(8,128)(2,1)}), bf16[32,16,64,128]{3,2,1,0:T(8,128)(2,1)}) %all-gather.2.cloned.1.call-update) | async-done | bytes 8388624 | tf_op jit(solution)/shard_map/all_gather | solution.py:42
  93.1 17.2 %shard_map.47 = f32[16,4,128,128]{3,2,1,0:T(8,128)} custom-call(bf16[4,128,2048]{2,1,0:T(8,128)(2,1)} %copy-done.2, bf16[16,4,2048]{2,1,0:T(4,128)(2,1)} %copy.10.mask_ref, bf16[32,16,64,128]{3,2,1,0:T(8,128)(2,1)} %all-gather.2.cloned.1.call-done.panel_ref), custom_call_target="tpu_custom_call" | custom-call | flops 4294967296 | bytes 15728640 | tf_op jit(solution)/shard_map/pallas_call | solution.py:63
  110.3 58.1 %all_to_all.5 = f32[16,4,128,128]{3,2,1,0:T(8,128)} all-to-all(f32[16,4,128,128]{3,2,1,0:T(8,128)} %shard_map.47), channel_id=1, replica_groups=mesh['row'=32,'col'=16] {'col'}, dimensions={0} | all-to-all | bytes 8388608 | tf_op jit(solution)/shard_map/all_to_all | solution.py:77
  168.5 3.1 %reduce_sum.9 = bf16[4,128,128]{2,1,0:T(8,128)(2,1)} reduce(f32[16,4,128,128]{3,2,1,0:T(8,128)} %all_to_all.5, f32[]{:T(128)} %constant.0.clone.1), dimensions={0}, to_apply=%region_0.0 | reduce | flops 983040 | bytes 4325380 | tf_op jit(solution)/shard_map/reduce_sum | solution.py:78
Async XLA Ops:
  6.5 5.5 %copy-start.1 = (s32[4,1,8]{2,1,0:T(1,128)S(1)}, s32[4,1,8]{2,1,0:T(1,128)}, u32[]{:S(2)}) copy-start(s32[4,1,8]{2,1,0:T(1,128)} %param.5) | copy-start | bytes 388
  6.5 5.5 %copy-start = (bf16[4,1,8,128,128]{4,3,2,1,0:T(8,128)(2,1)S(1)}, bf16[4,1,8,128,128]{4,3,2,1,0:T(8,128)(2,1)}, u32[]{:S(2)}) copy-start(bf16[4,1,8,128,128]{4,3,2,1,0:T(8,128)(2,1)} %param.4) | copy-start | bytes 3145732
  6.5 86.5 %all-gather.2.cloned.1.call-start = ((), (), s32[]{:S(2)}) async-start(), calls=%async_computation.1 | async-start | bytes 8650752 | tf_op jit(solution)/shard_map/all_gather | solution.py:42
  17.9 1.3 copy-start.2
Sparse Core Ops, SparseCore 0:
  9.5 83.5 all-gather.1

commit v2 on v0

v2 whole, which is shorter than its diff:
```python
import jax
import jax.numpy as jnp
from jax import lax
from jax.experimental import pallas as pl
from jax.experimental.pallas import tpu as pltpu
from jax.sharding import Mesh, PartitionSpec as P

ROWS = 32
NX = 4
NY = 4
NBC = 16
KFC = 8
SUB = 4
B = 128
CHUNK = NBC * SUB
PER_X = NY * CHUNK
SHARD = NX * PER_X
EXTRA = 16
MIB = 2**20


def code_kernel(shard_ref, code_ref):
    top = jnp.float32(0.0)
    for x in range(NX):
        top = jnp.maximum(top, jnp.max(jnp.abs(shard_ref[x, :PER_X].astype(jnp.float32))))
    lane = lax.broadcasted_iota(jnp.int32, (8, 128), 1)
    power = jnp.int32(126)
    scale = jnp.float32(2.0**126)
    for e in range(-96, 3):
        above = top >= jnp.float32(2.0**e)
        power = jnp.where(above, jnp.int32(29 - e), power)
        scale = jnp.where(above, jnp.float32(2.0 ** (29 - e)), scale)
    for x in range(NX):

        def step(t, carry):
            rows = pl.ds(pl.multiple_of(t * 16, 16), 16)
            value = shard_ref[x, rows].astype(jnp.float32) * scale
            size = jnp.abs(value)
            shift = jnp.zeros(value.shape, jnp.int32)
            down = jnp.ones(value.shape, jnp.float32)
            for s in range(1, 23):
                above = size >= jnp.float32(2.0 ** (7 + s))
                shift = jnp.where(above, jnp.int32(s * 512 + 256), shift)
                down = jnp.where(above, jnp.float32(2.0**-s), down)
            shift = jnp.where(shift == 0, 256, shift)
            mantissa = jnp.round(value * down).astype(jnp.int32)
            code_ref[pl.ds(pl.multiple_of(x * PER_X + t * 16, 16), 16)] = (shift + mantissa).astype(jnp.int16)
            return carry

        lax.fori_loop(0, PER_X // 16, step, 0)
    code_ref[SHARD:] = jnp.full((EXTRA, B), power, jnp.int32).astype(jnp.int16)


def product_kernel(y_ref, index_ref, keep_ref, factor_ref, panel_ref, *refs):
    out_refs, (block_ref, total_ref, scale_ref) = refs[:NY], refs[NY:]
    x = pl.program_id(0)
    y = y_ref[0]

    @pl.when(x == 0)
    def _():
        power = panel_ref[:, SHARD : SHARD + EXTRA].astype(jnp.int32)
        scale = jnp.ones(power.shape, jnp.float32)
        for bit in range(7):
            on = (power & (1 << bit)) > 0
            scale = scale * jnp.where(on, jnp.float32(2.0 ** -(1 << bit)), jnp.float32(1.0))
        scale_ref[...] = scale[:, :8]

    low = lax.broadcasted_iota(jnp.int32, (NBC // 2, 8, B), 1) < SUB

    def spread(q, carry):
        scales = [scale_ref[q * 4 + r] for r in range(4)]
        for t in range(NY):
            g = lax.rem(y + t, NY)
            rows = pl.ds(pl.multiple_of(x * PER_X + g * CHUNK, CHUNK), CHUNK)
            piece = []
            for r in range(4):
                code = panel_ref[q * 4 + r, rows].astype(jnp.int32)
                value = lax.shift_left((code & 511) - 256, lax.shift_right_logical(code, 9))
                piece.append(value.astype(jnp.float32).reshape(NBC // 2, 8, B) * scales[r])
            even, odd = [], []
            for a, b in ((piece[0], piece[1]), (piece[2], piece[3])):
                even.append(jnp.where(low, a, pltpu.roll(b, SUB, 1)))
                odd.append(jnp.where(low, pltpu.roll(a, SUB, 1), b))
            at = pl.ds(pl.multiple_of(q * 16, 16), 16)
            lanes = slice(t * B, (t + 1) * B)
            block_ref[:, 0, at, lanes] = jnp.concatenate(even, axis=1).astype(jnp.bfloat16)
            block_ref[:, 1, at, lanes] = jnp.concatenate(odd, axis=1).astype(jnp.bfloat16)
        return carry

    lax.fori_loop(0, ROWS // 4, spread, 0)

    n_i = total_ref.shape[0]

    def multiply(i, carry):
        total = jnp.zeros((B, NY * B), jnp.float32)
        for s in range(0, KFC, 2):
            left, right = [], []
            for u in (s, s + 1):
                left.append(factor_ref[0, i, u])
                k = index_ref[(x * n_i + i) * KFC + u]
                block = block_ref[k // 2, k % 2]
                kept = []
                for t in range(NY):
                    g = lax.rem(y + t, NY)
                    on = keep_ref[((x * n_i + i) * KFC + u) * NY + g] > 0
                    tile = block[:, t * B : (t + 1) * B]
                    kept.append(jnp.where(on, tile, jnp.zeros_like(tile)))
                right.append(jnp.concatenate(kept, axis=1))
            total += jnp.dot(
                jnp.concatenate(left, axis=1), jnp.concatenate(right, axis=0), preferred_element_type=jnp.float32
            )

        @pl.when(x == 0)
        def _():
            total_ref[i] = total

        @pl.when(x > 0)
        def _():
            total_ref[i] += total

        return carry

    lax.fori_loop(0, n_i, multiply, 0)

    @pl.when(x == NX - 1)
    def _():
        for t in range(NY):
            for i in range(n_i):
                out_refs[t][i] = total_ref[i, :, t * B : (t + 1) * B]


def per_device(factor, index, keep, panel):
    n_i = factor.shape[0]
    factor, index, keep = factor[:, 0], index[:, 0], keep[:, 0]
    y = lax.axis_index("y")

    factors = lax.all_gather(factor, "x", axis=0)

    shard = panel.reshape(NBC, NX, PER_X // CHUNK, SUB, B).transpose(1, 2, 0, 3, 4).reshape(NX, PER_X, B)
    small = jnp.concatenate(
        [
            jnp.broadcast_to(index[None], (NX, n_i, KFC)),
            keep.reshape(n_i, KFC, NX, NY).transpose(2, 0, 1, 3).reshape(NX, n_i, KFC * NY),
        ],
        axis=2,
    ).astype(jnp.bfloat16)
    small = jnp.pad(small, ((0, 0), (0, EXTRA - n_i), (0, B - KFC - KFC * NY)))
    mine = lax.all_to_all(jnp.concatenate([shard, small], axis=1), "x", 0, 0, tiled=True)
    small = mine[:, PER_X : PER_X + n_i].astype(jnp.int32)
    indices = small[:, :, :KFC].reshape(-1)
    keeps = small[:, :, KFC : KFC + KFC * NY].reshape(-1)

    code = pl.pallas_call(
        code_kernel,
        out_shape=jax.ShapeDtypeStruct((SHARD + EXTRA, B), jnp.int16),
        compiler_params=pltpu.CompilerParams(vmem_limit_bytes=32 * MIB),
    )(mine)
    gathered = lax.all_gather(code, ("z", "core"), axis=0)

    smem = pl.BlockSpec(memory_space=pltpu.SMEM)
    tile = jax.ShapeDtypeStruct((n_i, B, B), jnp.float32)
    parts = pl.pallas_call(
        product_kernel,
        grid=(NX,),
        in_specs=[
            smem,
            smem,
            smem,
            pl.BlockSpec((1, n_i, KFC, B, B), lambda x: (x, 0, 0, 0, 0)),
            pl.BlockSpec(memory_space=pltpu.VMEM),
        ],
        out_specs=[pl.BlockSpec((n_i, B, B), lambda x: (0, 0, 0))] * NY,
        out_shape=[tile] * NY,
        scratch_shapes=[
            pltpu.VMEM((NBC // 2, 2, B, NY * B), jnp.bfloat16),
            pltpu.VMEM((n_i, B, NY * B), jnp.float32),
            pltpu.VMEM((ROWS, 8, B), jnp.float32),
        ],
        compiler_params=pltpu.CompilerParams(vmem_limit_bytes=28 * MIB),
        cost_estimate=pl.CostEstimate(flops=2 * 2**30, bytes_accessed=13 * MIB, transcendentals=0),
    )(y.reshape(1), indices, keeps, factors, gathered)

    total = parts[0]
    for t in range(1, NY):
        total += lax.ppermute(parts[t], "y", [(i, (i + t) % NY) for i in range(NY)])
    return total.astype(jnp.bfloat16)[:, None]


def solution(mesh):
    fine = Mesh(mesh.devices.reshape(ROWS // 2, 2, NX, NY), ("z", "core", "x", "y"))
    row, col = ("z", "core"), ("x", "y")
    return jax.shard_map(
        per_device,
        mesh=fine,
        in_specs=(
            P(row, col, None, None, None),
            P(row, col, None),
            P(row, col, None, None),
            P(col, None, row, None),
        ),
        out_specs=P(row, col, None, None),
        check_vma=False,
    )
```

time: 296 us -> 139 us (0.47)
  the two profiles are of different devices: /device:TPU:2 before, /device:TPU:41 now
where the time goes in v2:
time: 139 us
  blocking collectives  69.5 us (50%)
  waiting for transfers between devices  17 us (12%)
  Pallas kernels  14.8 us (11%)
  starting transfers between devices  13.8 us (10%)
  between operations  13.5 us (10%)
  local copies, waits for them, and re-layouts  8.01 us (6%)
  other arithmetic  2.23 us (2%)
    all_gather x1, blocking collectives, per_device(): gathered = lax.all_gather(code, ('z', 'core'), axis=0)  69.5 us
    pallas_call x1, Pallas kernels, per_device(): pl.pallas_call(product_kernel, grid=(NX,), in_specs=[smem, smem, smem, pl...  12.7 us
    ppermute x3, waiting for transfers between devices, per_device(): total += lax.ppermute(parts[t], 'y', [(i, (i + t) % NY) for i in range(NY)])  10.6 us
    ppermute x3, starting transfers between devices, per_device(): total += lax.ppermute(parts[t], 'y', [(i, (i + t) % NY) for i in range(NY)])  9.81 us
    unnamed x6, local copies, waits for them, and re-layouts  6.4 us
    all_to_all x1, waiting for transfers between devices, per_device(): lax.all_to_all(jnp.concatenate([shard, small], axis=1), 'x', 0, 0, tiled=...  5.66 us
    all_to_all x1, starting transfers between devices, per_device(): lax.all_to_all(jnp.concatenate([shard, small], axis=1), 'x', 0, 0, tiled=...  4.01 us
  transfers between devices with their start and end apart: 5, of which 3 were waited for; matrix products, arithmetic and copies ran while one was open for 3% of the time, Pallas kernels for 1%

profile of v2, /device:TPU:41, one launch (start us, length us, event | category | flops | bytes accessed | tf_op | source)
XLA Modules:
  0.0 138.7 jit_solution(10750452390156704930)
XLA Ops:
  6.5 0.0 all-gather.5.cloned.1.call-start
  6.5 0.7 all-gather.5.cloned.1.call-update
  7.3 0.7 convert.12
  7.9 0.8 copy.13
  8.7 0.2 copy.14
  8.9 0.1 reshape.23
  9.0 1.1 copy.12
  10.1 0.1 fusion.6
  10.2 0.7 pad_maximum_fusion
  10.9 4.0 %all-to-all-start = ((bf16[4,272,128]{2,1,0:T(8,128)(2,1)}), bf16[4,272,128]{2,1,0:T(8,128)(2,1)S(1)}, u32[]{:S(2)}, u32[]{:S(2)}) async-start(bf16[4,272,128]{2,1,0:T(8,128)(2,1)} %pad_maximum_fusion), calls=%async_computation | async-start | bytes 557056 | tf_op jit(solution)/shard_map/all_to_all | solution.py:148
  14.9 5.7 %all-to-all-done.shard_ref = bf16[4,272,128]{2,1,0:T(8,128)(2,1)S(1)} async-done(((bf16[4,272,128]{2,1,0:T(8,128)(2,1)}), bf16[4,272,128]{2,1,0:T(8,128)(2,1)S(1)}, u32[]{:S(2)}, u32[]{:S(2)}) %all-to-all-start) | async-done | bytes 278560 | tf_op jit(solution)/shard_map/all_to_all | solution.py:148
  20.6 0.1 slice.14
  20.7 0.1 reshape.24.index_ref
  20.8 0.1 reshape.25.keep_ref
  20.9 2.1 %shard_map.46 = s16[1040,128]{1,0:T(8,128)(2,1)S(1)} custom-call(bf16[4,272,128]{2,1,0:T(8,128)(2,1)S(1)} %all-to-all-done.shard_ref), custom_call_target="tpu_custom_call" | custom-call | tf_op jit(solution)/shard_map/pallas_call | solution.py:153
  22.9 69.5 %all-gather.6 = s16[33280,128]{1,0:T(8,128)(2,1)} all-gather(s16[1040,128]{1,0:T(8,128)(2,1)S(1)} %shard_map.46), channel_id=3, replica_groups=mesh['z'=16,'core'=2,'x'=4,'y'=4] {'z','core'}, dimensions={0}, use_global_device_ids=true | all-gather | bytes 8785920 | tf_op jit(solution)/shard_map/all_gather | solution.py:158
  92.4 0.0 all-gather.5.cloned.1.call-done
  92.4 0.0 copy-start
  92.4 3.4 %copy-done = s16[33280,128]{1,0:T(8,128)(2,1)S(1)} copy-done((s16[33280,128]{1,0:T(8,128)(2,1)S(1)}, s16[33280,128]{1,0:T(8,128)(2,1)}, u32[]{:S(2)}) %copy-start) | copy-done | bytes 8519704
  95.8 0.0 copy-start.1
  95.8 2.2 %copy-done.1 = bf16[16,1,8,128,128]{4,3,2,1,0:T(8,128)(2,1)S(1)} copy-done((bf16[16,1,8,128,128]{4,3,2,1,0:T(8,128)(2,1)S(1)}, bf16[16,1,8,128,128]{4,3,2,1,0:T(8,128)(2,1)}, u32[]{:S(2)}) %copy-start.1) | copy-done | bytes 4194328
  98.0 12.7 %shard_map.47 = (f32[4,128,128]{2,1,0:T(8,128)S(1)}, f32[4,128,128]{2,1,0:T(8,128)S(1)}, f32[4,128,128]{2,1,0:T(8,128)S(1)}, f32[4,128,128]{2,1,0:T(8,128)S(1)}) custom-call(s32[1]{0:T(128)} %bitcast.y_ref, s32[128]{0:T(128)S(1)} %reshape.24.index_ref, s32[512]{0:T(512)S(1)} %reshape.25.keep_ref, bf16[4,4,8,128,128]{4,3,2,1,0:T(8,128)(2,1)S(1)} %bitcast.21, ...), custom_call_target="tpu_custom_call" | custom-call | flops 2147483648 | bytes 13631488 | tf_op jit(solution)/shard_map/pallas_call | solution.py:162
  110.7 3.2 %collective-permute-start = (f32[4,128,128]{2,1,0:T(8,128)S(1)}, f32[4,128,128]{2,1,0:T(8,128)S(1)}, u32[]{:S(2)}, u32[]{:S(2)}) collective-permute-start(f32[4,128,128]{2,1,0:T(8,128)S(1)} %get-tuple-element.10), channel_id=1, source_target_pairs={{0,1},{1,2},{2,3},{3,0},{4,5},{5,6},{6,7},{7,4},{8,9},{9,10},{10,1... | collective-permute-start | bytes 786440 | tf_op jit(solution)/shard_map/ppermute | solution.py:185
  113.9 2.6 %collective-permute-start.1 = (f32[4,128,128]{2,1,0:T(8,128)S(1)}, f32[4,128,128]{2,1,0:T(8,128)S(1)}, u32[]{:S(2)}, u32[]{:S(2)}) collective-permute-start(f32[4,128,128]{2,1,0:T(8,128)S(1)} %get-tuple-element.11), channel_id=1, source_target_pairs={{0,2},{1,3},{2,0},{3,1},{4,6},{5,7},{6,4},{7,5},{8,10},{9,11},{10,... | collective-permute-start | bytes 786440 | tf_op jit(solution)/shard_map/ppermute | solution.py:185
  116.6 4.0 %collective-permute-start.2 = (f32[4,128,128]{2,1,0:T(8,128)S(1)}, f32[4,128,128]{2,1,0:T(8,128)S(1)}, u32[]{:S(2)}, u32[]{:S(2)}) collective-permute-start(f32[4,128,128]{2,1,0:T(8,128)S(1)} %get-tuple-element.12), channel_id=1, source_target_pairs={{0,3},{1,0},{2,1},{3,2},{4,7},{5,4},{6,5},{7,6},{8,11},{9,8},{10,9... | collective-permute-start | bytes 786440 | tf_op jit(solution)/shard_map/ppermute | solution.py:185
  120.6 0.0 collective-permute-done
  120.6 4.3 %collective-permute-done.1 = f32[4,128,128]{2,1,0:T(8,128)S(1)} collective-permute-done((f32[4,128,128]{2,1,0:T(8,128)S(1)}, f32[4,128,128]{2,1,0:T(8,128)S(1)}, u32[]{:S(2)}, u32[]{:S(2)}) %collective-permute-start.1) | collective-permute-done | bytes 262176 | tf_op jit(solution)/shard_map/ppermute | solution.py:185
  124.8 6.4 %collective-permute-done.2 = f32[4,128,128]{2,1,0:T(8,128)S(1)} collective-permute-done((f32[4,128,128]{2,1,0:T(8,128)S(1)}, f32[4,128,128]{2,1,0:T(8,128)S(1)}, u32[]{:S(2)}, u32[]{:S(2)}) %collective-permute-start.2) | collective-permute-done | bytes 262176 | tf_op jit(solution)/shard_map/ppermute | solution.py:185
  131.2 0.7 fusion
  (4 shorter events, 0.0 us)
Async XLA Ops:
  6.5 85.9 %all-gather.5.cloned.1.call-start = ((), (), s32[]{:S(2)}) async-start(), calls=%async_computation.1 | async-start | bytes 5242880 | tf_op jit(solution)/shard_map/all_gather | solution.py:137
  10.9 9.7 %all-to-all-start = ((bf16[4,272,128]{2,1,0:T(8,128)(2,1)}), bf16[4,272,128]{2,1,0:T(8,128)(2,1)S(1)}, u32[]{:S(2)}, u32[]{:S(2)}) async-start(bf16[4,272,128]{2,1,0:T(8,128)(2,1)} %pad_maximum_fusion), calls=%async_computation | async-start | bytes 557056 | tf_op jit(solution)/shard_map/all_to_all | solution.py:148
  92.4 3.4 %copy-start = (s16[33280,128]{1,0:T(8,128)(2,1)S(1)}, s16[33280,128]{1,0:T(8,128)(2,1)}, u32[]{:S(2)}) copy-start(s16[33280,128]{1,0:T(8,128)(2,1)} %all-gather.6) | copy-start | bytes 25559044
  95.8 2.2 %copy-start.1 = (bf16[16,1,8,128,128]{4,3,2,1,0:T(8,128)(2,1)S(1)}, bf16[16,1,8,128,128]{4,3,2,1,0:T(8,128)(2,1)}, u32[]{:S(2)}) copy-start(bf16[16,1,8,128,128]{4,3,2,1,0:T(8,128)(2,1)} %all-gather.5.cloned.1.call-done) | copy-start | bytes 12582916
  110.7 9.8 %collective-permute-start = (f32[4,128,128]{2,1,0:T(8,128)S(1)}, f32[4,128,128]{2,1,0:T(8,128)S(1)}, u32[]{:S(2)}, u32[]{:S(2)}) collective-permute-start(f32[4,128,128]{2,1,0:T(8,128)S(1)} %get-tuple-element.10), channel_id=1, source_target_pairs={{0,1},{1,2},{2,3},{3,0},{4,5},{5,6},{6,7},{7,4},{8,9},{9,10},{10,1... | collective-permute-start | bytes 786440 | tf_op jit(solution)/shard_map/ppermute | solution.py:185
  113.9 10.9 %collective-permute-start.1 = (f32[4,128,128]{2,1,0:T(8,128)S(1)}, f32[4,128,128]{2,1,0:T(8,128)S(1)}, u32[]{:S(2)}, u32[]{:S(2)}) collective-permute-start(f32[4,128,128]{2,1,0:T(8,128)S(1)} %get-tuple-element.11), channel_id=1, source_target_pairs={{0,2},{1,3},{2,0},{3,1},{4,6},{5,7},{6,4},{7,5},{8,10},{9,11},{10,... | collective-permute-start | bytes 786440 | tf_op jit(solution)/shard_map/ppermute | solution.py:185
  116.6 14.6 %collective-permute-start.2 = (f32[4,128,128]{2,1,0:T(8,128)S(1)}, f32[4,128,128]{2,1,0:T(8,128)S(1)}, u32[]{:S(2)}, u32[]{:S(2)}) collective-permute-start(f32[4,128,128]{2,1,0:T(8,128)S(1)} %get-tuple-element.12), channel_id=1, source_target_pairs={{0,3},{1,0},{2,1},{3,2},{4,7},{5,4},{6,5},{7,6},{8,11},{9,8},{10,9... | collective-permute-start | bytes 786440 | tf_op jit(solution)/shard_map/ppermute | solution.py:185
Sparse Core Ops, SparseCore 0:
  9.5 59.9 all-gather.4

commit v3 on v2

v3 whole, which is shorter than its diff:
```python
import functools

import jax
import jax.numpy as jnp
from jax import lax
from jax.experimental import pallas as pl
from jax.experimental.pallas import tpu as pltpu
from jax.sharding import Mesh, PartitionSpec as P

ROWS = 32
NX = 4
NY = 4
NBC = 16
KFC = 8
SUB = 4
B = 128
CHUNK = NBC * SUB
PER_X = NY * CHUNK
SHARD = NX * PER_X
EXTRA = 16
MIB = 2**20


def code_kernel(shard_ref, code_ref):
    top = jnp.float32(0.0)
    for x in range(NX):
        top = jnp.maximum(top, jnp.max(jnp.abs(shard_ref[x, :PER_X].astype(jnp.float32))))
    lane = lax.broadcasted_iota(jnp.int32, (8, 128), 1)
    power = jnp.int32(126)
    scale = jnp.float32(2.0**126)
    for e in range(-96, 3):
        above = top >= jnp.float32(2.0**e)
        power = jnp.where(above, jnp.int32(29 - e), power)
        scale = jnp.where(above, jnp.float32(2.0 ** (29 - e)), scale)
    for x in range(NX):

        def step(t, carry):
            rows = pl.ds(pl.multiple_of(t * 16, 16), 16)
            value = shard_ref[x, rows].astype(jnp.float32) * scale
            size = jnp.abs(value)
            high = jnp.full(value.shape, 23 * 512, jnp.int32)
            down = jnp.ones(value.shape, jnp.float32)
            for s in range(1, 23):
                above = size >= jnp.float32(2.0 ** (7 + s))
                high = jnp.where(above, jnp.int32((23 - s) * 512), high)
                down = jnp.where(above, jnp.float32(2.0**-s), down)
            mantissa = jnp.round(value * down).astype(jnp.int32) & 511
            code_ref[pl.ds(pl.multiple_of(x * PER_X + t * 16, 16), 16)] = (high + mantissa).astype(jnp.int16)
            return carry

        lax.fori_loop(0, PER_X // 16, step, 0)
    code_ref[SHARD:] = jnp.full((EXTRA, B), power, jnp.int32).astype(jnp.int16)


def product_kernel(turns, place_ref, index_ref, keep_ref, *refs):
    n_t = len(turns)
    factor_refs, panel_ref, out_refs = refs[:NX], refs[NX], refs[NX + 1 : NX + 1 + n_t]
    code_ref, power_ref, scale_ref, block_a, block_b, sems, power_sem = refs[NX + 1 + n_t :]
    x, y = place_ref[0], place_ref[1]
    n_i = out_refs[0].shape[0]
    home = [lax.rem(x + NX - s, NX) for s in range(NX)]
    turn = [lax.rem(y + t, NY) for t in turns]

    copies = []
    for s in range(NX):
        for t in range(n_t):
            rows = pl.ds(pl.multiple_of(home[s] * PER_X + turn[t] * CHUNK, CHUNK), CHUNK)
            copies.append(pltpu.make_async_copy(panel_ref.at[:, rows], code_ref.at[s, t], sems.at[s, t]))
    powers = pltpu.make_async_copy(panel_ref.at[:, pl.ds(SHARD, EXTRA)], power_ref, power_sem)
    powers.start()
    for copy in copies:
        copy.start()
    for t in range(n_t):
        out_refs[t][...] = jnp.zeros_like(out_refs[t])
    powers.wait()
    power = power_ref[...].astype(jnp.int32)
    scale = jnp.ones(power.shape, jnp.float32)
    for bit in range(7):
        on = (power & (1 << bit)) > 0
        scale = scale * jnp.where(on, jnp.float32(2.0 ** -(1 << bit)), jnp.float32(1.0))
    scale_ref[...] = scale[:, :8]
    low = lax.broadcasted_iota(jnp.int32, (NBC // 2, 8, B), 1) < SUB

    def spread(s, q, block_ref):
        for t in range(n_t):
            piece = []
            for r in range(4):
                code = code_ref[s, t, q * 4 + r].astype(jnp.int32)
                value = lax.shift_right_arithmetic(lax.shift_left(code, 23), lax.shift_right_logical(code, 9))
                piece.append(value.astype(jnp.float32).reshape(NBC // 2, 8, B) * scale_ref[q * 4 + r])
            even, odd = [], []
            for a, b in ((piece[0], piece[1]), (piece[2], piece[3])):
                even.append(jnp.where(low, a, pltpu.roll(b, SUB, 1)))
                odd.append(jnp.where(low, pltpu.roll(a, SUB, 1), b))
            at = pl.ds(pl.multiple_of(q * 16, 16), 16)
            lanes = slice(t * B, (t + 1) * B)
            block_ref[:, 0, at, lanes] = jnp.concatenate(even, axis=1).astype(jnp.bfloat16)
            block_ref[:, 1, at, lanes] = jnp.concatenate(odd, axis=1).astype(jnp.bfloat16)

    def multiply(s, i, block_ref):
        total = jnp.zeros((B, n_t * B), jnp.float32)
        for u in range(0, KFC, 2):
            left, right = [], []
            for v in (u, u + 1):
                entry = (home[s] * n_i + i) * KFC + v
                left.append(factor_refs[s][i, v])
                k = index_ref[entry]
                block = block_ref[k // 2, k % 2]
                kept = []
                for t in range(n_t):
                    tile = block[:, t * B : (t + 1) * B]
                    kept.append(jnp.where(keep_ref[entry * NY + turn[t]] > 0, tile, jnp.zeros_like(tile)))
                right.append(jnp.concatenate(kept, axis=1))
            total += jnp.dot(
                jnp.concatenate(left, axis=1), jnp.concatenate(right, axis=0), preferred_element_type=jnp.float32
            )
        for t in range(n_t):
            out_refs[t][i] += total[:, t * B : (t + 1) * B]

    def arrive(s):
        for copy in copies[s * n_t : (s + 1) * n_t]:
            copy.wait()

    blocks = (block_a, block_b)
    arrive(0)

    def first(q, carry):
        spread(0, q, block_a)
        return carry

    lax.fori_loop(0, ROWS // 4, first, 0)
    for s in range(NX):
        if s + 1 < NX:
            arrive(s + 1)

        def step(i, carry, s=s):
            multiply(s, i, blocks[s % 2])
            if s + 1 < NX:
                for h in range(ROWS // 4 // n_i):
                    spread(s + 1, i * (ROWS // 4 // n_i) + h, blocks[(s + 1) % 2])
            return carry

        lax.fori_loop(0, n_i, step, 0)


def products(turns, place, indices, keeps, factors, gathered):
    n_i, n_t = factors[0].shape[0], len(turns)
    smem = pl.BlockSpec(memory_space=pltpu.SMEM)
    vmem = pl.BlockSpec(memory_space=pltpu.VMEM)
    return pl.pallas_call(
        functools.partial(product_kernel, turns),
        in_specs=[smem] * 3 + [vmem] * NX + [pl.BlockSpec(memory_space=pltpu.HBM)],
        out_specs=[vmem] * n_t,
        out_shape=[jax.ShapeDtypeStruct((n_i, B, B), jnp.float32)] * n_t,
        scratch_shapes=[
            pltpu.VMEM((NX, n_t, ROWS, CHUNK, B), jnp.int16),
            pltpu.VMEM((ROWS, EXTRA, B), jnp.int16),
            pltpu.VMEM((ROWS, 8, B), jnp.float32),
            pltpu.VMEM((NBC // 2, 2, B, n_t * B), jnp.bfloat16),
            pltpu.VMEM((NBC // 2, 2, B, n_t * B), jnp.bfloat16),
            pltpu.SemaphoreType.DMA((NX, n_t)),
            pltpu.SemaphoreType.DMA,
        ],
        compiler_params=pltpu.CompilerParams(vmem_limit_bytes=24 * MIB),
        cost_estimate=pl.CostEstimate(flops=n_t * 2**29, bytes_accessed=n_t * 3 * MIB, transcendentals=0),
    )(place, indices, keeps, *factors, gathered)


def per_device(factor, index, keep, panel):
    n_i = factor.shape[0]
    factor, index, keep = factor[:, 0], index[:, 0], keep[:, 0]
    place = jnp.stack([lax.axis_index("x"), lax.axis_index("y")]).astype(jnp.int32)

    factors = [factor]
    for s in range(1, NX):
        factors.append(lax.ppermute(factor, "x", [(i, (i + s) % NX) for i in range(NX)]))

    shard = panel.reshape(NBC, NX, PER_X // CHUNK, SUB, B).transpose(1, 2, 0, 3, 4).reshape(NX, PER_X, B)
    small = jnp.concatenate(
        [
            jnp.broadcast_to(index[None], (NX, n_i, KFC)),
            keep.reshape(n_i, KFC, NX, NY).transpose(2, 0, 1, 3).reshape(NX, n_i, KFC * NY),
        ],
        axis=2,
    ).astype(jnp.bfloat16)
    small = jnp.pad(small, ((0, 0), (0, EXTRA - n_i), (0, B - KFC - KFC * NY)))
    mine = lax.all_to_all(jnp.concatenate([shard, small], axis=1), "x", 0, 0, tiled=True)
    small = mine[:, PER_X : PER_X + n_i].astype(jnp.int32)
    indices = small[:, :, :KFC].reshape(-1)
    keeps = small[:, :, KFC : KFC + KFC * NY].reshape(-1)

    code = pl.pallas_call(
        code_kernel,
        out_shape=jax.ShapeDtypeStruct((SHARD + EXTRA, B), jnp.int16),
        compiler_params=pltpu.CompilerParams(vmem_limit_bytes=32 * MIB),
    )(mine)
    gathered = lax.all_gather(code, ("z", "core"), axis=0)
    parts = {}
    for turns in ((2,), (1, 3), (0,)):
        for t, part in zip(turns, products(turns, place, indices, keeps, factors, gathered)):
            parts[t] = lax.ppermute(part, "y", [(i, (i + t) % NY) for i in range(NY)]) if t else part
    total = parts[0] + parts[1] + parts[3] + parts[2]
    return total.astype(jnp.bfloat16)[:, None]


def solution(mesh):
    fine = Mesh(mesh.devices.reshape(ROWS // 2, 2, NX, NY), ("z", "core", "x", "y"))
    row, col = ("z", "core"), ("x", "y")
    return jax.shard_map(
        per_device,
        mesh=fine,
        in_specs=(
            P(row, col, None, None, None),
            P(row, col, None),
            P(row, col, None, None),
            P(col, None, row, None),
        ),
        out_specs=P(row, col, None, None),
        check_vma=False,
    )
```

time: 139 us -> 128 us (0.921)
  the two profiles are of different devices: /device:TPU:41 before, /device:TPU:32 now
where the time goes in v3:
time: 128 us
  blocking collectives  67.7 us (53%)
  starting transfers between devices  27.1 us (21%)
  Pallas kernels  23.8 us (19%)
  local copies, waits for them, and re-layouts  5.91 us (5%)
  other arithmetic  2.3 us (2%)
    all_gather x1, blocking collectives, per_device(): gathered = lax.all_gather(code, ('z', 'core'), axis=0)  67.7 us
    pallas_call x3, Pallas kernels, products(): pl.pallas_call(functools.partial(product_kernel, turns), in_specs=[smem]...  21.7 us
    ppermute x3, starting transfers between devices, per_device(): lax.ppermute(factor, 'x', [(i, (i + s) % NX) for i in range(NX)])  11.9 us
    ppermute x3, starting transfers between devices, per_device(): lax.ppermute(part, 'y', [(i, (i + t) % NY) for i in range(NY)])  11 us
    all_to_all x1, starting transfers between devices, per_device(): lax.all_to_all(jnp.concatenate([shard, small], axis=1), 'x', 0, 0, tiled=...  4.29 us
    unnamed x6, local copies, waits for them, and re-layouts  4.21 us
  transfers between devices with their start and end apart: 7, of which 1 were waited for; matrix products, arithmetic and copies ran while one was open for 0% of the time, Pallas kernels for 12%

profile of v3, /device:TPU:32, one launch (start us, length us, event | category | flops | bytes accessed | tf_op | source)
XLA Modules:
  0.0 127.9 jit_solution(4542169956394751582)
XLA Ops:
  0.0 1.2 copy.8
  1.2 0.8 copy.9
  2.0 0.2 copy.10
  2.1 0.1 reshape.19
  2.2 0.7 convert.12
  3.0 0.1 fusion.6
  3.0 0.7 pad_maximum_fusion
  3.8 4.3 %all-to-all-start = ((bf16[4,272,128]{2,1,0:T(8,128)(2,1)}), bf16[4,272,128]{2,1,0:T(8,128)(2,1)S(1)}, u32[]{:S(2)}, u32[]{:S(2)}) async-start(bf16[4,272,128]{2,1,0:T(8,128)(2,1)} %pad_maximum_fusion), calls=%async_computation | async-start | bytes 557056 | tf_op jit(solution)/shard_map/all_to_all | solution.py:187
  8.1 3.9 %collective-permute-start = (bf16[4,8,128,128]{3,2,1,0:T(8,128)(2,1)}, bf16[4,8,128,128]{3,2,1,0:T(8,128)(2,1)S(1)}, u32[]{:S(2)}, u32[]{:S(2)}) collective-permute-start(bf16[4,8,128,128]{3,2,1,0:T(8,128)(2,1)} %bitcast.24), channel_id=1, source_target_pairs={{0,4},{4,8},{8,12},{12,0},{1,5},{5,9},{9,13},{13,1},{2,6},{6,10},{... | collective-permute-start | bytes 3145736 | tf_op jit(solution)/shard_map/ppermute | solution.py:176
  12.0 4.6 %collective-permute-start.1 = (bf16[4,8,128,128]{3,2,1,0:T(8,128)(2,1)}, bf16[4,8,128,128]{3,2,1,0:T(8,128)(2,1)S(1)}, u32[]{:S(2)}, u32[]{:S(2)}) collective-permute-start(bf16[4,8,128,128]{3,2,1,0:T(8,128)(2,1)} %bitcast.25), channel_id=1, source_target_pairs={{0,8},{4,12},{8,0},{12,4},{1,9},{5,13},{9,1},{13,5},{2,10},{6,14},... | collective-permute-start | bytes 3145736 | tf_op jit(solution)/shard_map/ppermute | solution.py:176
  16.6 3.4 %collective-permute-start.2 = (bf16[4,8,128,128]{3,2,1,0:T(8,128)(2,1)}, bf16[4,8,128,128]{3,2,1,0:T(8,128)(2,1)}, u32[]{:S(2)}, u32[]{:S(2)}) collective-permute-start(bf16[4,8,128,128]{3,2,1,0:T(8,128)(2,1)} %bitcast.26), channel_id=1, source_target_pairs={{0,12},{4,0},{8,4},{12,8},{1,13},{5,1},{9,5},{13,9},{2,14},{6,2},{... | collective-permute-start | bytes 3145736 | tf_op jit(solution)/shard_map/ppermute | solution.py:176
  20.0 0.1 pad_add_fusion.place_ref
  20.0 0.0 all-to-all-done.shard_ref
  20.0 2.1 %shard_map.46 = s16[1040,128]{1,0:T(8,128)(2,1)S(1)} custom-call(bf16[4,272,128]{2,1,0:T(8,128)(2,1)S(1)} %all-to-all-done.shard_ref), custom_call_target="tpu_custom_call" | custom-call | tf_op jit(solution)/shard_map/pallas_call | solution.py:192
  22.2 67.7 %all-gather.2 = s16[33280,128]{1,0:T(8,128)(2,1)} all-gather(s16[1040,128]{1,0:T(8,128)(2,1)S(1)} %shard_map.46), channel_id=2, replica_groups=mesh['z'=16,'core'=2,'x'=4,'y'=4] {'z','core'}, dimensions={0}, use_global_device_ids=true | all-gather | bytes 8785920 | tf_op jit(solution)/shard_map/all_gather | solution.py:197
  89.9 0.1 slice.14
  89.9 0.1 reshape.21.keep_ref
  90.0 0.1 reshape.20.index_ref
  90.1 0.0 collective-permute-done.refs_1_
  90.1 0.0 collective-permute-done.1.refs_2_
  90.1 0.0 collective-permute-done.2.refs_3_
  90.2 3.4 %copy-done = s16[33280,128]{1,0:T(8,128)(2,1)S(1)} copy-done((s16[33280,128]{1,0:T(8,128)(2,1)S(1)}, s16[33280,128]{1,0:T(8,128)(2,1)}, u32[]{:S(2)}) %copy-start) | copy-done | bytes 8519704
  93.6 8.4 %shard_map.48 = (f32[4,128,128]{2,1,0:T(8,128)S(1)}, f32[4,128,128]{2,1,0:T(8,128)S(1)}) custom-call(s32[2]{0:T(128)S(1)} %pad_add_fusion.place_ref, s32[128]{0:T(128)S(1)} %reshape.20.index_ref, s32[512]{0:T(512)S(1)} %reshape.21.keep_ref, bf16[4,8,128,128]{3,2,1,0:T(8,128)(2,1)S(1)} %bitcast.27, bf16[4,8,128,128]{3,2,1,0:T(8,128)(2,1)S(1)} %collective-permute-done.refs_1_, ...), custom_call_target="tpu_custom_call" | custom-call | flops 1073741824 | bytes 6291456 | tf_op jit(solution)/shard_map/pallas_call | solution.py:150
  102.0 3.5 %collective-permute-start.3 = (f32[4,128,128]{2,1,0:T(8,128)S(1)}, f32[4,128,128]{2,1,0:T(8,128)S(1)}, u32[]{:S(2)}, u32[]{:S(2)}) collective-permute-start(f32[4,128,128]{2,1,0:T(8,128)S(1)} %get-tuple-element.7), channel_id=1, source_target_pairs={{0,1},{1,2},{2,3},{3,0},{4,5},{5,6},{6,7},{7,4},{8,9},{9,10},{10,1... | collective-permute-start | bytes 786440 | tf_op jit(solution)/shard_map/ppermute | solution.py:201
  105.5 3.6 %collective-permute-start.4 = (f32[4,128,128]{2,1,0:T(8,128)S(1)}, f32[4,128,128]{2,1,0:T(8,128)S(1)}, u32[]{:S(2)}, u32[]{:S(2)}) collective-permute-start(f32[4,128,128]{2,1,0:T(8,128)S(1)} %get-tuple-element.8), channel_id=1, source_target_pairs={{0,3},{1,0},{2,1},{3,2},{4,7},{5,4},{6,5},{7,6},{8,11},{9,8},{10,9... | collective-permute-start | bytes 786440 | tf_op jit(solution)/shard_map/ppermute | solution.py:201
  109.1 6.6 %shard_map.49 = f32[4,128,128]{2,1,0:T(8,128)S(1)} custom-call(s32[2]{0:T(128)S(1)} %pad_add_fusion.place_ref, s32[128]{0:T(128)S(1)} %reshape.20.index_ref, s32[512]{0:T(512)S(1)} %reshape.21.keep_ref, bf16[4,8,128,128]{3,2,1,0:T(8,128)(2,1)S(1)} %bitcast.28, bf16[4,8,128,128]{3,2,1,0:T(8,128)(2,1)S(1)} %collective-permute-done.refs_1_, ...), custom_call_target="tpu_custom_call" | custom-call | flops 536870912 | bytes 3145728 | tf_op jit(solution)/shard_map/pallas_call | solution.py:150
  115.7 3.9 %collective-permute-start.5 = (f32[4,128,128]{2,1,0:T(8,128)S(1)}, f32[4,128,128]{2,1,0:T(8,128)S(1)}, u32[]{:S(2)}, u32[]{:S(2)}) collective-permute-start(f32[4,128,128]{2,1,0:T(8,128)S(1)} %shard_map.49), channel_id=1, source_target_pairs={{0,2},{1,3},{2,0},{3,1},{4,6},{5,7},{6,4},{7,5},{8,10},{9,11},{10,... | collective-permute-start | bytes 786440 | tf_op jit(solution)/shard_map/ppermute | solution.py:201
  119.6 6.6 %shard_map.47 = f32[4,128,128]{2,1,0:T(8,128)S(1)} custom-call(s32[2]{0:T(128)S(1)} %pad_add_fusion.place_ref, s32[128]{0:T(128)S(1)} %reshape.20.index_ref, s32[512]{0:T(512)S(1)} %reshape.21.keep_ref, bf16[4,8,128,128]{3,2,1,0:T(8,128)(2,1)S(1)} %bitcast.29, bf16[4,8,128,128]{3,2,1,0:T(8,128)(2,1)S(1)} %collective-permute-done.refs_1_, ...), custom_call_target="tpu_custom_call" | custom-call | flops 536870912 | bytes 3145728 | tf_op jit(solution)/shard_map/pallas_call | solution.py:150
  126.2 0.0 collective-permute-done.3
  126.2 0.0 collective-permute-done.4
  126.3 0.9 collective-permute-done.5
  127.2 0.7 fusion
  (7 shorter events, 0.0 us)
Async XLA Ops:
  0.0 90.1 %copy-start.1 = (bf16[4,1,8,128,128]{4,3,2,1,0:T(8,128)(2,1)S(1)}, bf16[4,1,8,128,128]{4,3,2,1,0:T(8,128)(2,1)}, u32[]{:S(2)}) copy-start(bf16[4,1,8,128,128]{4,3,2,1,0:T(8,128)(2,1)} %param.4) | copy-start | bytes 3145732
  3.8 16.3 %all-to-all-start = ((bf16[4,272,128]{2,1,0:T(8,128)(2,1)}), bf16[4,272,128]{2,1,0:T(8,128)(2,1)S(1)}, u32[]{:S(2)}, u32[]{:S(2)}) async-start(bf16[4,272,128]{2,1,0:T(8,128)(2,1)} %pad_maximum_fusion), calls=%async_computation | async-start | bytes 557056 | tf_op jit(solution)/shard_map/all_to_all | solution.py:187
  8.1 82.1 %collective-permute-start = (bf16[4,8,128,128]{3,2,1,0:T(8,128)(2,1)}, bf16[4,8,128,128]{3,2,1,0:T(8,128)(2,1)S(1)}, u32[]{:S(2)}, u32[]{:S(2)}) collective-permute-start(bf16[4,8,128,128]{3,2,1,0:T(8,128)(2,1)} %bitcast.24), channel_id=1, source_target_pairs={{0,4},{4,8},{8,12},{12,0},{1,5},{5,9},{9,13},{13,1},{2,6},{6,10},{... | collective-permute-start | bytes 3145736 | tf_op jit(solution)/shard_map/ppermute | solution.py:176
  12.0 78.1 %collective-permute-start.1 = (bf16[4,8,128,128]{3,2,1,0:T(8,128)(2,1)}, bf16[4,8,128,128]{3,2,1,0:T(8,128)(2,1)S(1)}, u32[]{:S(2)}, u32[]{:S(2)}) collective-permute-start(bf16[4,8,128,128]{3,2,1,0:T(8,128)(2,1)} %bitcast.25), channel_id=1, source_target_pairs={{0,8},{4,12},{8,0},{12,4},{1,9},{5,13},{9,1},{13,5},{2,10},{6,14},... | collective-permute-start | bytes 3145736 | tf_op jit(solution)/shard_map/ppermute | solution.py:176
  16.6 73.6 %collective-permute-start.2 = (bf16[4,8,128,128]{3,2,1,0:T(8,128)(2,1)}, bf16[4,8,128,128]{3,2,1,0:T(8,128)(2,1)}, u32[]{:S(2)}, u32[]{:S(2)}) collective-permute-start(bf16[4,8,128,128]{3,2,1,0:T(8,128)(2,1)} %bitcast.26), channel_id=1, source_target_pairs={{0,12},{4,0},{8,4},{12,8},{1,13},{5,1},{9,5},{13,9},{2,14},{6,2},{... | collective-permute-start | bytes 3145736 | tf_op jit(solution)/shard_map/ppermute | solution.py:176
  90.2 3.4 %copy-start = (s16[33280,128]{1,0:T(8,128)(2,1)S(1)}, s16[33280,128]{1,0:T(8,128)(2,1)}, u32[]{:S(2)}) copy-start(s16[33280,128]{1,0:T(8,128)(2,1)} %all-gather.2) | copy-start | bytes 25559044
  102.0 24.2 %collective-permute-start.3 = (f32[4,128,128]{2,1,0:T(8,128)S(1)}, f32[4,128,128]{2,1,0:T(8,128)S(1)}, u32[]{:S(2)}, u32[]{:S(2)}) collective-permute-start(f32[4,128,128]{2,1,0:T(8,128)S(1)} %get-tuple-element.7), channel_id=1, source_target_pairs={{0,1},{1,2},{2,3},{3,0},{4,5},{5,6},{6,7},{7,4},{8,9},{9,10},{10,1... | collective-permute-start | bytes 786440 | tf_op jit(solution)/shard_map/ppermute | solution.py:201
  105.5 20.7 %collective-permute-start.4 = (f32[4,128,128]{2,1,0:T(8,128)S(1)}, f32[4,128,128]{2,1,0:T(8,128)S(1)}, u32[]{:S(2)}, u32[]{:S(2)}) collective-permute-start(f32[4,128,128]{2,1,0:T(8,128)S(1)} %get-tuple-element.8), channel_id=1, source_target_pairs={{0,3},{1,0},{2,1},{3,2},{4,7},{5,4},{6,5},{7,6},{8,11},{9,8},{10,9... | collective-permute-start | bytes 786440 | tf_op jit(solution)/shard_map/ppermute | solution.py:201
  115.7 11.5 %collective-permute-start.5 = (f32[4,128,128]{2,1,0:T(8,128)S(1)}, f32[4,128,128]{2,1,0:T(8,128)S(1)}, u32[]{:S(2)}, u32[]{:S(2)}) collective-permute-start(f32[4,128,128]{2,1,0:T(8,128)S(1)} %shard_map.49), channel_id=1, source_target_pairs={{0,2},{1,3},{2,0},{3,1},{4,6},{5,7},{6,4},{7,5},{8,10},{9,11},{10,... | collective-permute-start | bytes 786440 | tf_op jit(solution)/shard_map/ppermute | solution.py:201

commit v4 on v3

--- a/solution.py
+++ b/solution.py
@@ -52,26 +52,24 @@
     code_ref[SHARD:] = jnp.full((EXTRA, B), power, jnp.int32).astype(jnp.int16)
 
 
-def product_kernel(turns, place_ref, index_ref, keep_ref, *refs):
-    n_t = len(turns)
-    factor_refs, panel_ref, out_refs = refs[:NX], refs[NX], refs[NX + 1 : NX + 1 + n_t]
-    code_ref, power_ref, scale_ref, block_a, block_b, sems, power_sem = refs[NX + 1 + n_t :]
-    x, y = place_ref[0], place_ref[1]
-    n_i = out_refs[0].shape[0]
-    home = [lax.rem(x + NX - s, NX) for s in range(NX)]
+def product_kernel(turns, place_ref, index_ref, keep_ref, factors_ref, panel_ref, out_ref, *refs):
+    n_t, n_i = len(turns), factors_ref.shape[1]
+    code_ref, factor_ref, power_ref, scale_ref, block_a, block_b, sems, factor_sems, power_sem = refs
+    y = place_ref[0]
     turn = [lax.rem(y + t, NY) for t in turns]
+    slot = turn if out_ref.shape[0] == NY else [0]
 
     copies = []
-    for s in range(NX):
+    for x in range(NX):
         for t in range(n_t):
-            rows = pl.ds(pl.multiple_of(home[s] * PER_X + turn[t] * CHUNK, CHUNK), CHUNK)
-            copies.append(pltpu.make_async_copy(panel_ref.at[:, rows], code_ref.at[s, t], sems.at[s, t]))
+            rows = pl.ds(pl.multiple_of(x * PER_X + turn[t] * CHUNK, CHUNK), CHUNK)
+            copies.append(pltpu.make_async_copy(panel_ref.at[:, rows], code_ref.at[x, t], sems.at[x, t]))
+        copies.append(pltpu.make_async_copy(factors_ref.at[x], factor_ref.at[x], factor_sems.at[x]))
     powers = pltpu.make_async_copy(panel_ref.at[:, pl.ds(SHARD, EXTRA)], power_ref, power_sem)
     powers.start()
     for copy in copies:
         copy.start()
-    for t in range(n_t):
-        out_refs[t][...] = jnp.zeros_like(out_refs[t])
+    out_ref[...] = jnp.zeros_like(out_ref)
     powers.wait()
     power = power_ref[...].astype(jnp.int32)
     scale = jnp.ones(power.shape, jnp.float32)
@@ -81,11 +79,11 @@
     scale_ref[...] = scale[:, :8]
     low = lax.broadcasted_iota(jnp.int32, (NBC // 2, 8, B), 1) < SUB
 
-    def spread(s, q, block_ref):
+    def spread(x, q, block_ref):
         for t in range(n_t):
             piece = []
             for r in range(4):
-                code = code_ref[s, t, q * 4 + r].astype(jnp.int32)
+                code = code_ref[x, t, q * 4 + r].astype(jnp.int32)
                 value = lax.shift_right_arithmetic(lax.shift_left(code, 23), lax.shift_right_logical(code, 9))
                 piece.append(value.astype(jnp.float32).reshape(NBC // 2, 8, B) * scale_ref[q * 4 + r])
             even, odd = [], []
@@ -97,13 +95,13 @@
             block_ref[:, 0, at, lanes] = jnp.concatenate(even, axis=1).astype(jnp.bfloat16)
             block_ref[:, 1, at, lanes] = jnp.concatenate(odd, axis=1).astype(jnp.bfloat16)
 
-    def multiply(s, i, block_ref):
+    def multiply(x, i, block_ref):
         total = jnp.zeros((B, n_t * B), jnp.float32)
         for u in range(0, KFC, 2):
             left, right = [], []
             for v in (u, u + 1):
-                entry = (home[s] * n_i + i) * KFC + v
-                left.append(factor_refs[s][i, v])
+                entry = (x * n_i + i) * KFC + v
+                left.append(factor_ref[x, i, v])
                 k = index_ref[entry]
                 block = block_ref[k // 2, k % 2]
                 kept = []
@@ -115,10 +113,10 @@
                 jnp.concatenate(left, axis=1), jnp.concatenate(right, axis=0), preferred_element_type=jnp.float32
             )
         for t in range(n_t):
-            out_refs[t][i] += total[:, t * B : (t + 1) * B]
-
-    def arrive(s):
-        for copy in copies[s * n_t : (s + 1) * n_t]:
+            out_ref[slot[t], i] += total[:, t * B : (t + 1) * B]
+
+    def arrive(x):
+        for copy in copies[x * (n_t + 1) : (x + 1) * (n_t + 1)]:
             copy.wait()
 
     blocks = (block_a, block_b)
@@ -129,51 +127,48 @@
         return carry
 
     lax.fori_loop(0, ROWS // 4, first, 0)
-    for s in range(NX):
-        if s + 1 < NX:
-            arrive(s + 1)
-
-        def step(i, carry, s=s):
-            multiply(s, i, blocks[s % 2])
-            if s + 1 < NX:
-                for h in range(ROWS // 4 // n_i):
-                    spread(s + 1, i * (ROWS // 4 // n_i) + h, blocks[(s + 1) % 2])
-            return carry
-
-        lax.fori_loop(0, n_i, step, 0)
-
-
-def products(turns, place, indices, keeps, factors, gathered):
-    n_i, n_t = factors[0].shape[0], len(turns)
+    per_i = ROWS // 4 // n_i
+    for x in range(NX):
+        if x + 1 < NX:
+            arrive(x + 1)
+        for i in range(n_i):
+            multiply(x, i, blocks[x % 2])
+            if x + 1 < NX:
+                for h in range(per_i):
+                    spread(x + 1, i * per_i + h, blocks[(x + 1) % 2])
+
+
+def products(turns, n_out, place, indices, keeps, factors, gathered):
+    n_i, n_t = factors.shape[1], len(turns)
     smem = pl.BlockSpec(memory_space=pltpu.SMEM)
     vmem = pl.BlockSpec(memory_space=pltpu.VMEM)
     return pl.pallas_call(
         functools.partial(product_kernel, turns),
-        in_specs=[smem] * 3 + [vmem] * NX + [pl.BlockSpec(memory_space=pltpu.HBM)],
-        out_specs=[vmem] * n_t,
-        out_shape=[jax.ShapeDtypeStruct((n_i, B, B), jnp.float32)] * n_t,
+        in_specs=[smem] * 3 + [pl.BlockSpec(memory_space=pltpu.HBM)] * 2,
+        out_specs=vmem,
+        out_shape=jax.ShapeDtypeStruct((n_out, n_i, B, B), jnp.float32),
         scratch_shapes=[
             pltpu.VMEM((NX, n_t, ROWS, CHUNK, B), jnp.int16),
+            pltpu.VMEM(factors.shape, jnp.bfloat16),
             pltpu.VMEM((ROWS, EXTRA, B), jnp.int16),
             pltpu.VMEM((ROWS, 8, B), jnp.float32),
             pltpu.VMEM((NBC // 2, 2, B, n_t * B), jnp.bfloat16),
             pltpu.VMEM((NBC // 2, 2, B, n_t * B), jnp.bfloat16),
             pltpu.SemaphoreType.DMA((NX, n_t)),
+            pltpu.SemaphoreType.DMA((NX,)),
             pltpu.SemaphoreType.DMA,
         ],
-        compiler_params=pltpu.CompilerParams(vmem_limit_bytes=24 * MIB),
+        compiler_params=pltpu.CompilerParams(vmem_limit_bytes=56 * MIB),
         cost_estimate=pl.CostEstimate(flops=n_t * 2**29, bytes_accessed=n_t * 3 * MIB, transcendentals=0),
-    )(place, indices, keeps, *factors, gathered)
+    )(place, indices, keeps, factors, gathered)
 
 
 def per_device(factor, index, keep, panel):
     n_i = factor.shape[0]
     factor, index, keep = factor[:, 0], index[:, 0], keep[:, 0]
-    place = jnp.stack([lax.axis_index("x"), lax.axis_index("y")]).astype(jnp.int32)
-
-    factors = [factor]
-    for s in range(1, NX):
-        factors.append(lax.ppermute(factor, "x", [(i, (i + s) % NX) for i in range(NX)]))
+    place = lax.axis_index("y").astype(jnp.int32).reshape(1)
+
+    factors = lax.all_to_all(jnp.broadcast_to(factor[None], (NX,) + factor.shape), "x", 0, 0, tiled=True)
 
     shard = panel.reshape(NBC, NX, PER_X // CHUNK, SUB, B).transpose(1, 2, 0, 3, 4).reshape(NX, PER_X, B)
     small = jnp.concatenate(
@@ -195,11 +190,9 @@
         compiler_params=pltpu.CompilerParams(vmem_limit_bytes=32 * MIB),
     )(mine)
     gathered = lax.all_gather(code, ("z", "core"), axis=0)
-    parts = {}
-    for turns in ((2,), (1, 3), (0,)):
-        for t, part in zip(turns, products(turns, place, indices, keeps, factors, gathered)):
-            parts[t] = lax.ppermute(part, "y", [(i, (i + t) % NY) for i in range(NY)]) if t else part
-    total = parts[0] + parts[1] + parts[3] + parts[2]
+    args = (place, indices, keeps, factors, gathered)
+    others = lax.all_to_all(products((1, 2, 3), NY, *args), "y", 0, 0, tiled=True)
+    total = products((0,), 1, *args)[0] + others[0] + others[1] + others[2] + others[3]
     return total.astype(jnp.bfloat16)[:, None]
 
 

time: 128 us -> 131 us (1.023)
  the two profiles are of different devices: /device:TPU:32 before, /device:TPU:34 now
where the time goes in v4:
time: 131 us; the launch traced here: 130 us
  blocking collectives  67.8 us (52%)
  Pallas kernels  21.7 us (17%)
  starting transfers between devices  15.7 us (12%)
  waiting for transfers between devices  14.2 us (11%)
  local copies, waits for them, and re-layouts  7.7 us (6%)
  other arithmetic  3.17 us (2%)
    all_gather x1, blocking collectives, per_device(): gathered = lax.all_gather(code, ('z', 'core'), axis=0)  67.8 us
    pallas_call x2, Pallas kernels, products(): pl.pallas_call(functools.partial(product_kernel, turns), in_specs=[smem]...  19.6 us
    all_to_all x1, waiting for transfers between devices, per_device(): lax.all_to_all(products((1, 2, 3), NY, *args), 'y', 0, 0, tiled=True)  8.77 us
    all_to_all x1, starting transfers between devices, per_device(): lax.all_to_all(jnp.broadcast_to(factor[None], (NX,) + factor.shape), 'x',...  6.36 us
    all_to_all x1, waiting for transfers between devices, per_device(): lax.all_to_all(jnp.concatenate([shard, small], axis=1), 'x', 0, 0, tiled=...  5.39 us
    all_to_all x1, starting transfers between devices, per_device(): lax.all_to_all(jnp.concatenate([shard, small], axis=1), 'x', 0, 0, tiled=...  4.82 us
    all_to_all x1, starting transfers between devices, per_device(): lax.all_to_all(products((1, 2, 3), NY, *args), 'y', 0, 0, tiled=True)  4.49 us
    broadcast_in_dim x1, local copies, waits for them, and re-layouts, per_device(): jnp.broadcast_to(factor[None], (NX,) + factor.shape)  4.21 us
  transfers between devices with their start and end apart: 3, of which 2 were waited for; matrix products, arithmetic and copies ran while one was open for 1% of the time, Pallas kernels for 7%

profile of v4, /device:TPU:34, one launch (start us, length us, event | category | flops | bytes accessed | tf_op | source)
XLA Modules:
  0.0 130.2 jit_solution(16153313705600932324)
XLA Ops:
  0.0 0.7 convert.16
  0.7 0.8 copy.9
  1.5 0.2 copy.10
  1.7 0.1 reshape.79
  1.8 1.1 copy.8
  2.9 0.1 fusion.7
  2.9 0.7 pad_maximum_fusion
  3.7 4.8 %all-to-all-start = ((bf16[4,272,128]{2,1,0:T(8,128)(2,1)}), bf16[4,272,128]{2,1,0:T(8,128)(2,1)S(1)}, u32[]{:S(2)}, u32[]{:S(2)}) async-start(bf16[4,272,128]{2,1,0:T(8,128)(2,1)} %pad_maximum_fusion), calls=%async_computation | async-start | bytes 557056 | tf_op jit(solution)/shard_map/all_to_all | solution.py:182
  8.5 5.4 %all-to-all-done.shard_ref = bf16[4,272,128]{2,1,0:T(8,128)(2,1)S(1)} async-done(((bf16[4,272,128]{2,1,0:T(8,128)(2,1)}), bf16[4,272,128]{2,1,0:T(8,128)(2,1)S(1)}, u32[]{:S(2)}, u32[]{:S(2)}) %all-to-all-start) | async-done | bytes 278560 | tf_op jit(solution)/shard_map/all_to_all | solution.py:182
  13.9 4.2 %broadcast_in_dim.18 = bf16[4,4,8,128,128]{4,3,2,1,0:T(8,128)(2,1)} broadcast(bf16[4,8,128,128]{3,2,1,0:T(8,128)(2,1)} %bitcast.22), dimensions={1,2,3,4} | broadcast | bytes 5242880 | tf_op jit(solution)/shard_map/broadcast_in_dim | solution.py:171
  18.1 6.4 %all-to-all-start.1 = ((bf16[4,4,8,128,128]{4,3,2,1,0:T(8,128)(2,1)}), bf16[4,4,8,128,128]{4,3,2,1,0:T(8,128)(2,1)}, u32[]{:S(2)}, u32[]{:S(2)}) async-start(bf16[4,4,8,128,128]{4,3,2,1,0:T(8,128)(2,1)} %broadcast_in_dim.18), calls=%async_computation.1 | async-start | bytes 8388608 | tf_op jit(solution)/shard_map/all_to_all | solution.py:171
  24.4 0.1 slice.30
  24.5 0.6 reshape.80.index_ref
  25.1 0.7 reshape.81.keep_ref
  25.8 2.1 %shard_map.46 = s16[1040,128]{1,0:T(8,128)(2,1)S(1)} custom-call(bf16[4,272,128]{2,1,0:T(8,128)(2,1)S(1)} %all-to-all-done.shard_ref), custom_call_target="tpu_custom_call" | custom-call | tf_op jit(solution)/shard_map/pallas_call | solution.py:187
  27.9 67.8 %all-gather.2 = s16[33280,128]{1,0:T(8,128)(2,1)} all-gather(s16[1040,128]{1,0:T(8,128)(2,1)S(1)} %shard_map.46), channel_id=2, replica_groups=mesh['z'=16,'core'=2,'x'=4,'y'=4] {'z','core'}, dimensions={0}, use_global_device_ids=true | all-gather | bytes 8785920 | tf_op jit(solution)/shard_map/all_gather | solution.py:192
  95.7 0.0 all-to-all-done.1.factors_ref
  95.7 12.7 %shard_map.48 = f32[4,4,128,128]{3,2,1,0:T(8,128)} custom-call(s32[1]{0:T(128)} %bitcast.place_ref, s32[128]{0:T(128)} %reshape.80.index_ref, s32[512]{0:T(512)} %reshape.81.keep_ref, bf16[4,4,8,128,128]{4,3,2,1,0:T(8,128)(2,1)} %all-to-all-done.1.factors_ref, s16[32,1040,128]{2,1,0:T(8,128)(2,1)} %bitcast.20), custom_call_target="tpu_custom_call" | custom-call | flops 1610612736 | bytes 9437184 | tf_op jit(solution)/shard_map/pallas_call | solution.py:145
  108.4 4.5 %all-to-all-start.2 = ((f32[4,4,128,128]{3,2,1,0:T(8,128)}), f32[4,4,128,128]{3,2,1,0:T(8,128)S(1)}, u32[]{:S(2)}, u32[]{:S(2)}) async-start(f32[4,4,128,128]{3,2,1,0:T(8,128)} %shard_map.48), calls=%async_computation.2 | async-start | bytes 2097152 | tf_op jit(solution)/shard_map/all_to_all | solution.py:194
  112.9 6.8 %shard_map.47 = f32[1,4,128,128]{3,2,1,0:T(8,128)} custom-call(s32[1]{0:T(128)} %bitcast.place_ref, s32[128]{0:T(128)} %reshape.80.index_ref, s32[512]{0:T(512)} %reshape.81.keep_ref, bf16[4,4,8,128,128]{4,3,2,1,0:T(8,128)(2,1)} %all-to-all-done.1.factors_ref, s16[32,1040,128]{2,1,0:T(8,128)(2,1)} %bitcast.21), custom_call_target="tpu_custom_call" | custom-call | flops 536870912 | bytes 3145728 | tf_op jit(solution)/shard_map/pallas_call | solution.py:145
  119.7 8.8 %all-to-all-done.2 = f32[4,4,128,128]{3,2,1,0:T(8,128)S(1)} async-done(((f32[4,4,128,128]{3,2,1,0:T(8,128)}), f32[4,4,128,128]{3,2,1,0:T(8,128)S(1)}, u32[]{:S(2)}, u32[]{:S(2)}) %all-to-all-start.2) | async-done | bytes 1048608 | tf_op jit(solution)/shard_map/all_to_all | solution.py:194
  128.5 1.7 %fusion.1 = bf16[4,1,128,128]{3,2,1,0:T(8,128)(2,1)} fusion(f32[4,4,128,128]{3,2,1,0:T(8,128)S(1)} %all-to-all-done.2, f32[1,4,128,128]{3,2,1,0:T(8,128)} %shard_map.47), kind=kLoop, calls=%fused_computation.6 | loop fusion | flops 327680 | bytes 1441792 | tf_op jit(solution)/shard_map/add | solution.py:195
  (4 shorter events, 0.0 us)
Async XLA Ops:
  3.7 10.2 %all-to-all-start = ((bf16[4,272,128]{2,1,0:T(8,128)(2,1)}), bf16[4,272,128]{2,1,0:T(8,128)(2,1)S(1)}, u32[]{:S(2)}, u32[]{:S(2)}) async-start(bf16[4,272,128]{2,1,0:T(8,128)(2,1)} %pad_maximum_fusion), calls=%async_computation | async-start | bytes 557056 | tf_op jit(solution)/shard_map/all_to_all | solution.py:182
  18.1 77.6 %all-to-all-start.1 = ((bf16[4,4,8,128,128]{4,3,2,1,0:T(8,128)(2,1)}), bf16[4,4,8,128,128]{4,3,2,1,0:T(8,128)(2,1)}, u32[]{:S(2)}, u32[]{:S(2)}) async-start(bf16[4,4,8,128,128]{4,3,2,1,0:T(8,128)(2,1)} %broadcast_in_dim.18), calls=%async_computation.1 | async-start | bytes 8388608 | tf_op jit(solution)/shard_map/all_to_all | solution.py:171
  108.4 20.1 %all-to-all-start.2 = ((f32[4,4,128,128]{3,2,1,0:T(8,128)}), f32[4,4,128,128]{3,2,1,0:T(8,128)S(1)}, u32[]{:S(2)}, u32[]{:S(2)}) async-start(f32[4,4,128,128]{3,2,1,0:T(8,128)} %shard_map.48), calls=%async_computation.2 | async-start | bytes 2097152 | tf_op jit(solution)/shard_map/all_to_all | solution.py:194

commit v5 on v3

v5 whole, which is shorter than its diff:
```python
import functools

import jax
import jax.numpy as jnp
from jax import lax
from jax.experimental import pallas as pl
from jax.experimental.pallas import tpu as pltpu
from jax.sharding import Mesh, PartitionSpec as P

ROWS = 32
NX = 4
NY = 4
NBC = 16
KFC = 8
SUB = 4
B = 128
CHUNK = NBC * SUB
PER_X = NY * CHUNK
SHARD = NX * PER_X
EXTRA = 16
MIB = 2**20


def code_kernel(shard_ref, code_ref, small_ref):
    top = jnp.float32(0.0)
    for x in range(NX):
        top = jnp.maximum(top, jnp.max(jnp.abs(shard_ref[x, :PER_X].astype(jnp.float32))))
    lane = lax.broadcasted_iota(jnp.int32, (8, 128), 1)
    power = jnp.int32(126)
    scale = jnp.float32(2.0**126)
    for e in range(-96, 3):
        above = top >= jnp.float32(2.0**e)
        power = jnp.where(above, jnp.int32(29 - e), power)
        scale = jnp.where(above, jnp.float32(2.0 ** (29 - e)), scale)
    for x in range(NX):

        def step(t, carry):
            rows = pl.ds(pl.multiple_of(t * 16, 16), 16)
            value = shard_ref[x, rows].astype(jnp.float32) * scale
            size = jnp.abs(value)
            high = jnp.full(value.shape, 23 * 512, jnp.int32)
            down = jnp.ones(value.shape, jnp.float32)
            for s in range(1, 23):
                above = size >= jnp.float32(2.0 ** (7 + s))
                high = jnp.where(above, jnp.int32((23 - s) * 512), high)
                down = jnp.where(above, jnp.float32(2.0**-s), down)
            mantissa = jnp.round(value * down).astype(jnp.int32) & 511
            code_ref[pl.ds(pl.multiple_of(x * PER_X + t * 16, 16), 16)] = (high + mantissa).astype(jnp.int16)
            return carry

        lax.fori_loop(0, PER_X // 16, step, 0)
    small_ref[...] = shard_ref[:, PER_X:].astype(jnp.int32).reshape(NX * EXTRA, B)
    code_ref[SHARD:] = jnp.full((EXTRA, B), power, jnp.int32).astype(jnp.int16)


def product_kernel(turns, place_ref, small_ref, *refs):
    n_t = len(turns)
    factor_refs, panel_ref, out_refs = refs[:NX], refs[NX], refs[NX + 1 : NX + 1 + n_t]
    code_ref, power_ref, scale_ref, block_a, block_b, sems, power_sem = refs[NX + 1 + n_t :]
    n_i = factor_refs[0].shape[0]
    x, y = place_ref[0], place_ref[1]
    home = [lax.rem(x + NX - s, NX) for s in range(NX)]
    turn = [lax.rem(y + t, NY) for t in turns]

    copies = []
    for s in range(NX):
        for t in range(n_t):
            rows = pl.ds(pl.multiple_of(home[s] * PER_X + turn[t] * CHUNK, CHUNK), CHUNK)
            copies.append(pltpu.make_async_copy(panel_ref.at[:, rows], code_ref.at[s, t], sems.at[s, t]))
    powers = pltpu.make_async_copy(panel_ref.at[:, pl.ds(SHARD, EXTRA)], power_ref, power_sem)
    powers.start()
    for copy in copies:
        copy.start()
    powers.wait()
    power = power_ref[...].astype(jnp.int32)
    scale = jnp.ones(power.shape, jnp.float32)
    for bit in range(7):
        on = (power & (1 << bit)) > 0
        scale = scale * jnp.where(on, jnp.float32(2.0 ** -(1 << bit)), jnp.float32(1.0))
    scale_ref[...] = scale[:, :8]
    low = lax.broadcasted_iota(jnp.int32, (NBC // 2, 8, B), 1) < SUB

    def spread(s, q, t, block_ref):
        piece = []
        for r in range(4):
            code = code_ref[s, t, q * 4 + r].astype(jnp.int32)
            value = lax.shift_right_arithmetic(lax.shift_left(code, 23), lax.shift_right_logical(code, 9))
            piece.append(value.astype(jnp.float32).reshape(NBC // 2, 8, B) * scale_ref[q * 4 + r])
        even, odd = [], []
        for a, b in ((piece[0], piece[1]), (piece[2], piece[3])):
            even.append(jnp.where(low, a, pltpu.roll(b, SUB, 1)))
            odd.append(jnp.where(low, pltpu.roll(a, SUB, 1), b))
        at = pl.ds(pl.multiple_of(q * 16, 16), 16)
        lanes = slice(t * B, (t + 1) * B)
        block_ref[:, 0, at, lanes] = jnp.concatenate(even, axis=1).astype(jnp.bfloat16)
        block_ref[:, 1, at, lanes] = jnp.concatenate(odd, axis=1).astype(jnp.bfloat16)

    def multiply(s, i, u, block_ref):
        left, right = [], []
        for v in (u, u + 1):
            row = home[s] * EXTRA + i
            left.append(factor_refs[s][i, v])
            k = small_ref[row, v]
            block = block_ref[k // 2, k % 2]
            kept = []
            for t in range(n_t):
                tile = block[:, t * B : (t + 1) * B]
                kept.append(jnp.where(small_ref[row, KFC + v * NY + turn[t]] > 0, tile, jnp.zeros_like(tile)))
            right.append(jnp.concatenate(kept, axis=1))
        return jnp.dot(
            jnp.concatenate(left, axis=1), jnp.concatenate(right, axis=0), preferred_element_type=jnp.float32
        )

    def arrive(s):
        for copy in copies[s * n_t : (s + 1) * n_t]:
            copy.wait()

    blocks = (block_a, block_b)
    arrive(0)

    def first(q, carry):
        for t in range(n_t):
            spread(0, q, t, block_a)
        return carry

    lax.fori_loop(0, ROWS // 4, first, 0)
    for s in range(NX):
        pieces = [(q, t) for q in range(ROWS // 4) for t in range(n_t)] if s + 1 < NX else []
        if s + 1 < NX:
            arrive(s + 1)
        for i in range(n_i):
            total = None
            for u in range(0, KFC, 2):
                part = multiply(s, i, u, blocks[s % 2])
                total = part if total is None else total + part
                n = i * (KFC // 2) + u // 2
                n_dots = n_i * KFC // 2
                for q, t in pieces[len(pieces) * n // n_dots : len(pieces) * (n + 1) // n_dots]:
                    spread(s + 1, q, t, blocks[(s + 1) % 2])
            for t in range(n_t):
                part = total[:, t * B : (t + 1) * B]
                out_refs[t][i] = part if s == 0 else out_refs[t][i] + part


def products(turns, place, small, factors, gathered):
    n_i, n_t = factors[0].shape[0], len(turns)
    smem = pl.BlockSpec(memory_space=pltpu.SMEM)
    vmem = pl.BlockSpec(memory_space=pltpu.VMEM)
    return pl.pallas_call(
        functools.partial(product_kernel, turns),
        in_specs=[smem] * 2 + [vmem] * NX + [pl.BlockSpec(memory_space=pltpu.HBM)],
        out_specs=[vmem] * n_t,
        out_shape=[jax.ShapeDtypeStruct((n_i, B, B), jnp.float32)] * n_t,
        scratch_shapes=[
            pltpu.VMEM((NX, n_t, ROWS, CHUNK, B), jnp.int16),
            pltpu.VMEM((ROWS, EXTRA, B), jnp.int16),
            pltpu.VMEM((ROWS, 8, B), jnp.float32),
            pltpu.VMEM((NBC // 2, 2, B, n_t * B), jnp.bfloat16),
            pltpu.VMEM((NBC // 2, 2, B, n_t * B), jnp.bfloat16),
            pltpu.SemaphoreType.DMA((NX, n_t)),
            pltpu.SemaphoreType.DMA,
        ],
        compiler_params=pltpu.CompilerParams(vmem_limit_bytes=47 * MIB),
        cost_estimate=pl.CostEstimate(flops=n_t * 2**29, bytes_accessed=n_t * 3 * MIB, transcendentals=0),
    )(place, small, *factors, gathered)


def per_device(factor, index, keep, panel):
    n_i = factor.shape[0]
    factor, index, keep = factor[:, 0], index[:, 0], keep[:, 0]
    place = jnp.stack([lax.axis_index("x"), lax.axis_index("y")]).astype(jnp.int32)

    factors = [factor]
    for s in range(1, NX):
        factors.append(lax.ppermute(factor, "x", [(i, (i + s) % NX) for i in range(NX)]))

    shard = panel.reshape(NBC, NX, PER_X // CHUNK, SUB, B).transpose(1, 2, 0, 3, 4).reshape(NX, PER_X, B)
    small = jnp.concatenate(
        [
            jnp.broadcast_to(index[None], (NX, n_i, KFC)),
            keep.reshape(n_i, KFC, NX, NY).transpose(2, 0, 1, 3).reshape(NX, n_i, KFC * NY),
        ],
        axis=2,
    ).astype(jnp.bfloat16)
    small = jnp.pad(small, ((0, 0), (0, EXTRA - n_i), (0, B - KFC - KFC * NY)))
    mine = lax.all_to_all(jnp.concatenate([shard, small], axis=1), "x", 0, 0, tiled=True)

    code, small = pl.pallas_call(
        code_kernel,
        out_shape=[
            jax.ShapeDtypeStruct((SHARD + EXTRA, B), jnp.int16),
            jax.ShapeDtypeStruct((NX * EXTRA, B), jnp.int32),
        ],
        compiler_params=pltpu.CompilerParams(vmem_limit_bytes=32 * MIB),
    )(mine)
    gathered = lax.all_gather(code, ("z", "core"), axis=0)
    args = (place, small, factors, gathered)
    away = []
    for t, part in zip((2, 1, 3), products((2, 1, 3), *args)):
        away.append(lax.ppermute(part, "y", [(i, (i + t) % NY) for i in range(NY)]))
    total = products((0,), *args)[0] + away[0] + away[1] + away[2]
    return total.astype(jnp.bfloat16)[:, None]


def solution(mesh):
    fine = Mesh(mesh.devices.reshape(ROWS // 2, 2, NX, NY), ("z", "core", "x", "y"))
    row, col = ("z", "core"), ("x", "y")
    return jax.shard_map(
        per_device,
        mesh=fine,
        in_specs=(
            P(row, col, None, None, None),
            P(row, col, None),
            P(row, col, None, None),
            P(col, None, row, None),
        ),
        out_specs=P(row, col, None, None),
        check_vma=False,
    )
```

time: 128 us -> 127 us (level)
  the two profiles are of different devices: /device:TPU:32 before, /device:TPU:37 now
where the time goes in v5:
time: 127 us
  blocking collectives  79.2 us (62%)
  starting transfers between devices  21.1 us (17%)
  Pallas kernels  18.6 us (15%)
  waiting for transfers between devices  3.06 us (2%)
  other arithmetic  2.38 us (2%)
  local copies, waits for them, and re-layouts  2.15 us (2%)
    all_gather x1, blocking collectives, per_device(): gathered = lax.all_gather(code, ('z', 'core'), axis=0)  79.2 us
    pallas_call x2, Pallas kernels, products(): pl.pallas_call(functools.partial(product_kernel, turns), in_specs=[smem]...  16.5 us
    ppermute x3, starting transfers between devices, per_device(): away.append(lax.ppermute(part, 'y', [(i, (i + t) % NY) for i in range(NY)]))  8.41 us
    ppermute x3, starting transfers between devices, per_device(): lax.ppermute(factor, 'x', [(i, (i + s) % NX) for i in range(NX)])  8.41 us
    all_to_all x1, starting transfers between devices, per_device(): lax.all_to_all(jnp.concatenate([shard, small], axis=1), 'x', 0, 0, tiled=...  4.24 us
    ppermute x3, waiting for transfers between devices, per_device(): away.append(lax.ppermute(part, 'y', [(i, (i + t) % NY) for i in range(NY)]))  3.05 us
  transfers between devices with their start and end apart: 7, of which 1 were waited for; matrix products, arithmetic and copies ran while one was open for 0% of the time, Pallas kernels for 6%

profile of v5, /device:TPU:37, one launch (start us, length us, event | category | flops | bytes accessed | tf_op | source)
XLA Modules:
  0.0 126.6 jit_solution(13924487737235651438)
XLA Ops:
  0.0 0.0 copy-start
  0.0 0.8 convert.12
  0.8 0.8 copy.9
  1.6 0.2 copy.10
  1.8 0.1 reshape.13
  1.9 1.1 copy.8
  3.0 0.1 fusion.6
  3.0 0.7 pad_maximum_fusion
  3.8 4.2 %all-to-all-start = ((bf16[4,272,128]{2,1,0:T(8,128)(2,1)}), bf16[4,272,128]{2,1,0:T(8,128)(2,1)S(1)}, u32[]{:S(2)}, u32[]{:S(2)}) async-start(bf16[4,272,128]{2,1,0:T(8,128)(2,1)} %pad_maximum_fusion), calls=%async_computation | async-start | bytes 557056 | tf_op jit(solution)/shard_map/all_to_all | solution.py:186
  8.0 2.2 %collective-permute-start.2 = (bf16[4,8,128,128]{3,2,1,0:T(8,128)(2,1)}, bf16[4,8,128,128]{3,2,1,0:T(8,128)(2,1)S(1)}, u32[]{:S(2)}, u32[]{:S(2)}) collective-permute-start(bf16[4,8,128,128]{3,2,1,0:T(8,128)(2,1)} %bitcast.20), channel_id=1, source_target_pairs={{0,12},{4,0},{8,4},{12,8},{1,13},{5,1},{9,5},{13,9},{2,14},{6,2},{... | collective-permute-start | bytes 3145736 | tf_op jit(solution)/shard_map/ppermute | solution.py:175
  10.2 4.3 %collective-permute-start.1 = (bf16[4,8,128,128]{3,2,1,0:T(8,128)(2,1)}, bf16[4,8,128,128]{3,2,1,0:T(8,128)(2,1)S(1)}, u32[]{:S(2)}, u32[]{:S(2)}) collective-permute-start(bf16[4,8,128,128]{3,2,1,0:T(8,128)(2,1)} %bitcast.21), channel_id=1, source_target_pairs={{0,8},{4,12},{8,0},{12,4},{1,9},{5,13},{9,1},{13,5},{2,10},{6,14},... | collective-permute-start | bytes 3145736 | tf_op jit(solution)/shard_map/ppermute | solution.py:175
  14.5 1.9 %collective-permute-start = (bf16[4,8,128,128]{3,2,1,0:T(8,128)(2,1)}, bf16[4,8,128,128]{3,2,1,0:T(8,128)(2,1)}, u32[]{:S(2)}, u32[]{:S(2)}) collective-permute-start(bf16[4,8,128,128]{3,2,1,0:T(8,128)(2,1)} %bitcast.22), channel_id=1, source_target_pairs={{0,4},{4,8},{8,12},{12,0},{1,5},{5,9},{9,13},{13,1},{2,6},{6,10},{... | collective-permute-start | bytes 3145736 | tf_op jit(solution)/shard_map/ppermute | solution.py:175
  16.4 0.1 pad_add_fusion.place_ref
  16.5 0.0 all-to-all-done.shard_ref
  16.5 2.1 %shard_map.46 = (s16[1040,128]{1,0:T(8,128)(2,1)S(1)}, s32[64,128]{1,0:T(8,128)S(1)}) custom-call(bf16[4,272,128]{2,1,0:T(8,128)(2,1)S(1)} %all-to-all-done.shard_ref), custom_call_target="tpu_custom_call" | custom-call | tf_op jit(solution)/shard_map/pallas_call | solution.py:188
  18.6 79.2 %all-gather.2 = s16[33280,128]{1,0:T(8,128)(2,1)} all-gather(s16[1040,128]{1,0:T(8,128)(2,1)S(1)} %get-tuple-element.11), channel_id=2, replica_groups=mesh['z'=16,'core'=2,'x'=4,'y'=4] {'z','core'}, dimensions={0}, use_global_device_ids=true | all-gather | bytes 8785920 | tf_op jit(solution)/shard_map/all_gather | solution.py:196
  97.8 0.0 collective-permute-done.2.refs_3_
  97.9 0.0 collective-permute-done.1.refs_2_
  97.9 0.0 collective-permute-done.refs_1_
  97.9 0.0 copy-done
  97.9 10.7 %shard_map.48 = (f32[4,128,128]{2,1,0:T(8,128)S(1)}, f32[4,128,128]{2,1,0:T(8,128)S(1)}, f32[4,128,128]{2,1,0:T(8,128)S(1)}) custom-call(s32[2]{0:T(128)S(1)} %pad_add_fusion.place_ref, s32[64,128]{1,0:T(8,128)S(1)} %get-tuple-element.10.small_ref, bf16[4,8,128,128]{3,2,1,0:T(8,128)(2,1)S(1)} %bitcast.23, ...), custom_call_target="tpu_custom_call" | custom-call | flops 1610612736 | bytes 9437184 | tf_op jit(solution)/shard_map/pallas_call | solution.py:149
  108.6 1.9 %collective-permute-start.3 = (f32[4,128,128]{2,1,0:T(8,128)S(1)}, f32[4,128,128]{2,1,0:T(8,128)S(1)}, u32[]{:S(2)}, u32[]{:S(2)}) collective-permute-start(f32[4,128,128]{2,1,0:T(8,128)S(1)} %get-tuple-element.12), channel_id=1, source_target_pairs={{0,2},{1,3},{2,0},{3,1},{4,6},{5,7},{6,4},{7,5},{8,10},{9,11},{10,... | collective-permute-start | bytes 786440 | tf_op jit(solution)/shard_map/ppermute | solution.py:200
  110.5 1.9 %collective-permute-start.4 = (f32[4,128,128]{2,1,0:T(8,128)S(1)}, f32[4,128,128]{2,1,0:T(8,128)S(1)}, u32[]{:S(2)}, u32[]{:S(2)}) collective-permute-start(f32[4,128,128]{2,1,0:T(8,128)S(1)} %get-tuple-element.13), channel_id=1, source_target_pairs={{0,1},{1,2},{2,3},{3,0},{4,5},{5,6},{6,7},{7,4},{8,9},{9,10},{10,1... | collective-permute-start | bytes 786440 | tf_op jit(solution)/shard_map/ppermute | solution.py:200
  112.4 4.6 %collective-permute-start.5 = (f32[4,128,128]{2,1,0:T(8,128)S(1)}, f32[4,128,128]{2,1,0:T(8,128)S(1)}, u32[]{:S(2)}, u32[]{:S(2)}) collective-permute-start(f32[4,128,128]{2,1,0:T(8,128)S(1)} %get-tuple-element.14), channel_id=1, source_target_pairs={{0,3},{1,0},{2,1},{3,2},{4,7},{5,4},{6,5},{7,6},{8,11},{9,8},{10,9... | collective-permute-start | bytes 786440 | tf_op jit(solution)/shard_map/ppermute | solution.py:200
  117.0 5.8 %shard_map.47 = f32[4,128,128]{2,1,0:T(8,128)S(1)} custom-call(s32[2]{0:T(128)S(1)} %pad_add_fusion.place_ref, s32[64,128]{1,0:T(8,128)S(1)} %get-tuple-element.10.small_ref, bf16[4,8,128,128]{3,2,1,0:T(8,128)(2,1)S(1)} %bitcast.24, bf16[4,8,128,128]{3,2,1,0:T(8,128)(2,1)} %collective-permute-done.refs_1_, ...), custom_call_target="tpu_custom_call" | custom-call | flops 536870912 | bytes 3145728 | tf_op jit(solution)/shard_map/pallas_call | solution.py:149
  122.8 0.0 collective-permute-done.3
  122.8 3.0 %collective-permute-done.4 = f32[4,128,128]{2,1,0:T(8,128)S(1)} collective-permute-done((f32[4,128,128]{2,1,0:T(8,128)S(1)}, f32[4,128,128]{2,1,0:T(8,128)S(1)}, u32[]{:S(2)}, u32[]{:S(2)}) %collective-permute-start.4) | collective-permute-done | bytes 262176 | tf_op jit(solution)/shard_map/ppermute | solution.py:200
  125.9 0.0 collective-permute-done.5
  125.9 0.7 fusion
  (3 shorter events, 0.0 us)
Async XLA Ops:
  0.0 97.9 %copy-start = (bf16[4,1,8,128,128]{4,3,2,1,0:T(8,128)(2,1)S(1)}, bf16[4,1,8,128,128]{4,3,2,1,0:T(8,128)(2,1)}, u32[]{:S(2)}) copy-start(bf16[4,1,8,128,128]{4,3,2,1,0:T(8,128)(2,1)} %param.4) | copy-start | bytes 3145732
  3.8 12.8 %all-to-all-start = ((bf16[4,272,128]{2,1,0:T(8,128)(2,1)}), bf16[4,272,128]{2,1,0:T(8,128)(2,1)S(1)}, u32[]{:S(2)}, u32[]{:S(2)}) async-start(bf16[4,272,128]{2,1,0:T(8,128)(2,1)} %pad_maximum_fusion), calls=%async_computation | async-start | bytes 557056 | tf_op jit(solution)/shard_map/all_to_all | solution.py:186
  8.0 89.8 %collective-permute-start.2 = (bf16[4,8,128,128]{3,2,1,0:T(8,128)(2,1)}, bf16[4,8,128,128]{3,2,1,0:T(8,128)(2,1)S(1)}, u32[]{:S(2)}, u32[]{:S(2)}) collective-permute-start(bf16[4,8,128,128]{3,2,1,0:T(8,128)(2,1)} %bitcast.20), channel_id=1, source_target_pairs={{0,12},{4,0},{8,4},{12,8},{1,13},{5,1},{9,5},{13,9},{2,14},{6,2},{... | collective-permute-start | bytes 3145736 | tf_op jit(solution)/shard_map/ppermute | solution.py:175
  10.2 87.7 %collective-permute-start.1 = (bf16[4,8,128,128]{3,2,1,0:T(8,128)(2,1)}, bf16[4,8,128,128]{3,2,1,0:T(8,128)(2,1)S(1)}, u32[]{:S(2)}, u32[]{:S(2)}) collective-permute-start(bf16[4,8,128,128]{3,2,1,0:T(8,128)(2,1)} %bitcast.21), channel_id=1, source_target_pairs={{0,8},{4,12},{8,0},{12,4},{1,9},{5,13},{9,1},{13,5},{2,10},{6,14},... | collective-permute-start | bytes 3145736 | tf_op jit(solution)/shard_map/ppermute | solution.py:175
  14.5 83.4 %collective-permute-start = (bf16[4,8,128,128]{3,2,1,0:T(8,128)(2,1)}, bf16[4,8,128,128]{3,2,1,0:T(8,128)(2,1)}, u32[]{:S(2)}, u32[]{:S(2)}) collective-permute-start(bf16[4,8,128,128]{3,2,1,0:T(8,128)(2,1)} %bitcast.22), channel_id=1, source_target_pairs={{0,4},{4,8},{8,12},{12,0},{1,5},{5,9},{9,13},{13,1},{2,6},{6,10},{... | collective-permute-start | bytes 3145736 | tf_op jit(solution)/shard_map/ppermute | solution.py:175
  108.6 14.2 %collective-permute-start.3 = (f32[4,128,128]{2,1,0:T(8,128)S(1)}, f32[4,128,128]{2,1,0:T(8,128)S(1)}, u32[]{:S(2)}, u32[]{:S(2)}) collective-permute-start(f32[4,128,128]{2,1,0:T(8,128)S(1)} %get-tuple-element.12), channel_id=1, source_target_pairs={{0,2},{1,3},{2,0},{3,1},{4,6},{5,7},{6,4},{7,5},{8,10},{9,11},{10,... | collective-permute-start | bytes 786440 | tf_op jit(solution)/shard_map/ppermute | solution.py:200
  110.5 15.4 %collective-permute-start.4 = (f32[4,128,128]{2,1,0:T(8,128)S(1)}, f32[4,128,128]{2,1,0:T(8,128)S(1)}, u32[]{:S(2)}, u32[]{:S(2)}) collective-permute-start(f32[4,128,128]{2,1,0:T(8,128)S(1)} %get-tuple-element.13), channel_id=1, source_target_pairs={{0,1},{1,2},{2,3},{3,0},{4,5},{5,6},{6,7},{7,4},{8,9},{9,10},{10,1... | collective-permute-start | bytes 786440 | tf_op jit(solution)/shard_map/ppermute | solution.py:200
  112.4 13.4 %collective-permute-start.5 = (f32[4,128,128]{2,1,0:T(8,128)S(1)}, f32[4,128,128]{2,1,0:T(8,128)S(1)}, u32[]{:S(2)}, u32[]{:S(2)}) collective-permute-start(f32[4,128,128]{2,1,0:T(8,128)S(1)} %get-tuple-element.14), channel_id=1, source_target_pairs={{0,3},{1,0},{2,1},{3,2},{4,7},{5,4},{6,5},{7,6},{8,11},{9,8},{10,9... | collective-permute-start | bytes 786440 | tf_op jit(solution)/shard_map/ppermute | solution.py:200

commit v6 on v5

--- a/solution.py
+++ b/solution.py
@@ -18,7 +18,29 @@
 PER_X = NY * CHUNK
 SHARD = NX * PER_X
 EXTRA = 16
+META = 32
 MIB = 2**20
+
+
+def pack_kernel(panel_hbm, index_hbm, keep_hbm, out_ref, panel_ref, index_ref, keep_ref, sems):
+    pairs = ((panel_hbm, panel_ref), (index_hbm, index_ref), (keep_hbm, keep_ref))
+    copies = [pltpu.make_async_copy(a, b, sems.at[n]) for n, (a, b) in enumerate(pairs)]
+    for copy in copies:
+        copy.start()
+    for copy in copies:
+        copy.wait()
+    for g in range(NX * NY):
+        rows = panel_ref[:, g].astype(jnp.float32).reshape(CHUNK, B)
+        out_ref[g // NY, (g % NY) * CHUNK : (g % NY + 1) * CHUNK] = rows.astype(jnp.bfloat16)
+    index = jnp.concatenate(
+        [jnp.broadcast_to(index_ref[i : i + 1], (KFC, KFC)) for i in range(META // KFC)], axis=0
+    )
+    own = lax.broadcasted_iota(jnp.int32, (META, KFC), 0) % KFC == lax.broadcasted_iota(jnp.int32, (META, KFC), 1)
+    index = jnp.sum(jnp.where(own, index.astype(jnp.float32), 0.0), axis=1, keepdims=True)
+    for x in range(NX):
+        out_ref[x, PER_X:] = jnp.zeros((META, B), jnp.bfloat16)
+        out_ref[x, PER_X:, : NX * NY] = keep_ref[...].astype(jnp.float32).astype(jnp.bfloat16)
+        out_ref[x, PER_X:, NX * NY : NX * NY + 1] = index.astype(jnp.bfloat16)
 
 
 def code_kernel(shard_ref, code_ref, small_ref):
@@ -37,19 +59,17 @@
         def step(t, carry):
             rows = pl.ds(pl.multiple_of(t * 16, 16), 16)
             value = shard_ref[x, rows].astype(jnp.float32) * scale
-            size = jnp.abs(value)
             high = jnp.full(value.shape, 23 * 512, jnp.int32)
-            down = jnp.ones(value.shape, jnp.float32)
-            for s in range(1, 23):
-                above = size >= jnp.float32(2.0 ** (7 + s))
-                high = jnp.where(above, jnp.int32((23 - s) * 512), high)
-                down = jnp.where(above, jnp.float32(2.0**-s), down)
-            mantissa = jnp.round(value * down).astype(jnp.int32) & 511
+            for s in (16, 8, 4, 2, 1):
+                above = jnp.abs(value) >= jnp.float32(2.0 ** (7 + s))
+                high = jnp.where(above, high - s * 512, high)
+                value = jnp.where(above, value * jnp.float32(2.0**-s), value)
+            mantissa = jnp.round(value).astype(jnp.int32) & 511
             code_ref[pl.ds(pl.multiple_of(x * PER_X + t * 16, 16), 16)] = (high + mantissa).astype(jnp.int16)
             return carry
 
         lax.fori_loop(0, PER_X // 16, step, 0)
-    small_ref[...] = shard_ref[:, PER_X:].astype(jnp.int32).reshape(NX * EXTRA, B)
+    small_ref[...] = shard_ref[:, PER_X:].astype(jnp.int32).reshape(NX * META, B)
     code_ref[SHARD:] = jnp.full((EXTRA, B), power, jnp.int32).astype(jnp.int16)
 
 
@@ -98,14 +118,14 @@
     def multiply(s, i, u, block_ref):
         left, right = [], []
         for v in (u, u + 1):
-            row = home[s] * EXTRA + i
+            row = home[s] * META + i * KFC + v
             left.append(factor_refs[s][i, v])
-            k = small_ref[row, v]
+            k = small_ref[row, NX * NY]
             block = block_ref[k // 2, k % 2]
             kept = []
             for t in range(n_t):
                 tile = block[:, t * B : (t + 1) * B]
-                kept.append(jnp.where(small_ref[row, KFC + v * NY + turn[t]] > 0, tile, jnp.zeros_like(tile)))
+                kept.append(jnp.where(small_ref[row, x * NY + turn[t]] > 0, tile, jnp.zeros_like(tile)))
             right.append(jnp.concatenate(kept, axis=1))
         return jnp.dot(
             jnp.concatenate(left, axis=1), jnp.concatenate(right, axis=0), preferred_element_type=jnp.float32
@@ -174,22 +194,25 @@
     for s in range(1, NX):
         factors.append(lax.ppermute(factor, "x", [(i, (i + s) % NX) for i in range(NX)]))
 
-    shard = panel.reshape(NBC, NX, PER_X // CHUNK, SUB, B).transpose(1, 2, 0, 3, 4).reshape(NX, PER_X, B)
-    small = jnp.concatenate(
-        [
-            jnp.broadcast_to(index[None], (NX, n_i, KFC)),
-            keep.reshape(n_i, KFC, NX, NY).transpose(2, 0, 1, 3).reshape(NX, n_i, KFC * NY),
+    packed = pl.pallas_call(
+        pack_kernel,
+        in_specs=[pl.BlockSpec(memory_space=pltpu.HBM)] * 3,
+        out_shape=jax.ShapeDtypeStruct((NX, PER_X + META, B), jnp.bfloat16),
+        scratch_shapes=[
+            pltpu.VMEM(panel.shape, jnp.bfloat16),
+            pltpu.VMEM(index.shape, jnp.int32),
+            pltpu.VMEM((n_i * KFC, NX * NY), jnp.int32),
+            pltpu.SemaphoreType.DMA((3,)),
         ],
-        axis=2,
-    ).astype(jnp.bfloat16)
-    small = jnp.pad(small, ((0, 0), (0, EXTRA - n_i), (0, B - KFC - KFC * NY)))
-    mine = lax.all_to_all(jnp.concatenate([shard, small], axis=1), "x", 0, 0, tiled=True)
+        compiler_params=pltpu.CompilerParams(vmem_limit_bytes=63 * MIB),
+    )(panel, index, keep.reshape(n_i * KFC, NX * NY))
+    mine = lax.all_to_all(packed, "x", 0, 0, tiled=True)
 
     code, small = pl.pallas_call(
         code_kernel,
         out_shape=[
             jax.ShapeDtypeStruct((SHARD + EXTRA, B), jnp.int16),
-            jax.ShapeDtypeStruct((NX * EXTRA, B), jnp.int32),
+            jax.ShapeDtypeStruct((NX * META, B), jnp.int32),
         ],
         compiler_params=pltpu.CompilerParams(vmem_limit_bytes=32 * MIB),
     )(mine)

time: 127 us -> 125 us (0.984)
  local copies, waits for them, and re-layouts: 2.15 us -> 0.01 us
  Pallas kernels: 18.6 us -> 20.5 us
  other arithmetic: 2.38 us -> 0.79 us
    pallas_call x0 -> x1, Pallas kernels: none -> 1.78 us  [per_device(): pl.pallas_call(pack_kernel, in_specs=[pl.BlockSpec(memory_space=pltpu.HBM...]
where the time goes in v6:
time: 125 us
  blocking collectives  79.4 us (64%)
  starting transfers between devices  21.2 us (17%)
  Pallas kernels  20.5 us (16%)
  waiting for transfers between devices  2.64 us (2%)
    all_gather x1, blocking collectives, per_device(): gathered = lax.all_gather(code, ('z', 'core'), axis=0)  79.4 us
    pallas_call x2, Pallas kernels, products(): pl.pallas_call(functools.partial(product_kernel, turns), in_specs=[smem]...  17.3 us
    ppermute x3, starting transfers between devices, per_device(): away.append(lax.ppermute(part, 'y', [(i, (i + t) % NY) for i in range(NY)]))  8.41 us
    ppermute x3, starting transfers between devices, per_device(): lax.ppermute(factor, 'x', [(i, (i + s) % NX) for i in range(NX)])  8.41 us
    all_to_all x1, starting transfers between devices, per_device(): mine = lax.all_to_all(packed, 'x', 0, 0, tiled=True)  4.38 us
    ppermute x3, waiting for transfers between devices, per_device(): away.append(lax.ppermute(part, 'y', [(i, (i + t) % NY) for i in range(NY)]))  2.63 us
  transfers between devices with their start and end apart: 7, of which 1 were waited for; matrix products, arithmetic and copies ran while one was open for 0% of the time, Pallas kernels for 6%

profile of v6, /device:TPU:37, one launch (start us, length us, event | category | flops | bytes accessed | tf_op | source)
XLA Modules:
  0.0 124.6 jit_solution(17903426705298747435)
XLA Ops:
  0.0 1.8 %shard_map.46 = bf16[4,288,128]{2,1,0:T(8,128)(2,1)} custom-call(bf16[16,16,4,128]{3,2,1,0:T(4,128)(2,1)} %panel_hbm.1, s32[4,8]{1,0:T(4,128)} %bitcast.18, s32[32,16]{1,0:T(8,128)} %bitcast.17), custom_call_target="tpu_custom_call" | custom-call | tf_op jit(solution)/shard_map/pallas_call | solution.py:197
  1.8 0.0 copy-start
  1.8 4.4 %all-to-all-start = ((bf16[4,288,128]{2,1,0:T(8,128)(2,1)}), bf16[4,288,128]{2,1,0:T(8,128)(2,1)S(1)}, u32[]{:S(2)}, u32[]{:S(2)}) async-start(bf16[4,288,128]{2,1,0:T(8,128)(2,1)} %shard_map.46), calls=%async_computation | async-start | bytes 589824 | tf_op jit(solution)/shard_map/all_to_all | solution.py:209
  6.2 2.2 %collective-permute-start.2 = (bf16[4,8,128,128]{3,2,1,0:T(8,128)(2,1)}, bf16[4,8,128,128]{3,2,1,0:T(8,128)(2,1)S(1)}, u32[]{:S(2)}, u32[]{:S(2)}) collective-permute-start(bf16[4,8,128,128]{3,2,1,0:T(8,128)(2,1)} %bitcast.10), channel_id=1, source_target_pairs={{0,12},{4,0},{8,4},{12,8},{1,13},{5,1},{9,5},{13,9},{2,14},{6,2},{... | collective-permute-start | bytes 3145736 | tf_op jit(solution)/shard_map/ppermute | solution.py:195
  8.4 4.3 %collective-permute-start.1 = (bf16[4,8,128,128]{3,2,1,0:T(8,128)(2,1)}, bf16[4,8,128,128]{3,2,1,0:T(8,128)(2,1)S(1)}, u32[]{:S(2)}, u32[]{:S(2)}) collective-permute-start(bf16[4,8,128,128]{3,2,1,0:T(8,128)(2,1)} %bitcast.11), channel_id=1, source_target_pairs={{0,8},{4,12},{8,0},{12,4},{1,9},{5,13},{9,1},{13,5},{2,10},{6,14},... | collective-permute-start | bytes 3145736 | tf_op jit(solution)/shard_map/ppermute | solution.py:195
  12.7 1.9 %collective-permute-start = (bf16[4,8,128,128]{3,2,1,0:T(8,128)(2,1)}, bf16[4,8,128,128]{3,2,1,0:T(8,128)(2,1)}, u32[]{:S(2)}, u32[]{:S(2)}) collective-permute-start(bf16[4,8,128,128]{3,2,1,0:T(8,128)(2,1)} %bitcast.12), channel_id=1, source_target_pairs={{0,4},{4,8},{8,12},{12,0},{1,5},{5,9},{9,13},{13,1},{2,6},{6,10},{... | collective-permute-start | bytes 3145736 | tf_op jit(solution)/shard_map/ppermute | solution.py:195
  14.6 0.1 pad_add_fusion.place_ref
  14.7 0.0 all-to-all-done.shard_ref
  14.7 1.4 %shard_map.47 = (s16[1040,128]{1,0:T(8,128)(2,1)S(1)}, s32[128,128]{1,0:T(8,128)S(1)}) custom-call(bf16[4,288,128]{2,1,0:T(8,128)(2,1)S(1)} %all-to-all-done.shard_ref), custom_call_target="tpu_custom_call" | custom-call | tf_op jit(solution)/shard_map/pallas_call | solution.py:211
  16.1 79.4 %all-gather.2 = s16[33280,128]{1,0:T(8,128)(2,1)} all-gather(s16[1040,128]{1,0:T(8,128)(2,1)S(1)} %get-tuple-element.11), channel_id=2, replica_groups=mesh['z'=16,'core'=2,'x'=4,'y'=4] {'z','core'}, dimensions={0}, use_global_device_ids=true | all-gather | bytes 8785920 | tf_op jit(solution)/shard_map/all_gather | solution.py:219
  95.5 0.0 collective-permute-done.2.refs_3_
  95.5 0.0 collective-permute-done.1.refs_2_
  95.5 0.0 collective-permute-done.refs_1_
  95.5 0.0 copy-done
  95.5 11.1 %shard_map.49 = (f32[4,128,128]{2,1,0:T(8,128)S(1)}, f32[4,128,128]{2,1,0:T(8,128)S(1)}, f32[4,128,128]{2,1,0:T(8,128)S(1)}) custom-call(s32[2]{0:T(128)S(1)} %pad_add_fusion.place_ref, s32[128,128]{1,0:T(8,128)S(1)} %get-tuple-element.10.small_ref, bf16[4,8,128,128]{3,2,1,0:T(8,128)(2,1)S(1)} %bitcast.13, ...), custom_call_target="tpu_custom_call" | custom-call | flops 1610612736 | bytes 9437184 | tf_op jit(solution)/shard_map/pallas_call | solution.py:169
  106.6 1.9 %collective-permute-start.3 = (f32[4,128,128]{2,1,0:T(8,128)S(1)}, f32[4,128,128]{2,1,0:T(8,128)S(1)}, u32[]{:S(2)}, u32[]{:S(2)}) collective-permute-start(f32[4,128,128]{2,1,0:T(8,128)S(1)} %get-tuple-element.12), channel_id=1, source_target_pairs={{0,2},{1,3},{2,0},{3,1},{4,6},{5,7},{6,4},{7,5},{8,10},{9,11},{10,... | collective-permute-start | bytes 786440 | tf_op jit(solution)/shard_map/ppermute | solution.py:223
  108.5 1.9 %collective-permute-start.4 = (f32[4,128,128]{2,1,0:T(8,128)S(1)}, f32[4,128,128]{2,1,0:T(8,128)S(1)}, u32[]{:S(2)}, u32[]{:S(2)}) collective-permute-start(f32[4,128,128]{2,1,0:T(8,128)S(1)} %get-tuple-element.13), channel_id=1, source_target_pairs={{0,1},{1,2},{2,3},{3,0},{4,5},{5,6},{6,7},{7,4},{8,9},{9,10},{10,1... | collective-permute-start | bytes 786440 | tf_op jit(solution)/shard_map/ppermute | solution.py:223
  110.5 4.6 %collective-permute-start.5 = (f32[4,128,128]{2,1,0:T(8,128)S(1)}, f32[4,128,128]{2,1,0:T(8,128)S(1)}, u32[]{:S(2)}, u32[]{:S(2)}) collective-permute-start(f32[4,128,128]{2,1,0:T(8,128)S(1)} %get-tuple-element.14), channel_id=1, source_target_pairs={{0,3},{1,0},{2,1},{3,2},{4,7},{5,4},{6,5},{7,6},{8,11},{9,8},{10,9... | collective-permute-start | bytes 786440 | tf_op jit(solution)/shard_map/ppermute | solution.py:223
  115.1 6.2 %shard_map.48 = f32[4,128,128]{2,1,0:T(8,128)S(1)} custom-call(s32[2]{0:T(128)S(1)} %pad_add_fusion.place_ref, s32[128,128]{1,0:T(8,128)S(1)} %get-tuple-element.10.small_ref, bf16[4,8,128,128]{3,2,1,0:T(8,128)(2,1)S(1)} %bitcast.14, bf16[4,8,128,128]{3,2,1,0:T(8,128)(2,1)} %collective-permute-done.refs_1_, ...), custom_call_target="tpu_custom_call" | custom-call | flops 536870912 | bytes 3145728 | tf_op jit(solution)/shard_map/pallas_call | solution.py:169
  121.3 0.0 collective-permute-done.3
  121.3 2.6 %collective-permute-done.4 = f32[4,128,128]{2,1,0:T(8,128)S(1)} collective-permute-done((f32[4,128,128]{2,1,0:T(8,128)S(1)}, f32[4,128,128]{2,1,0:T(8,128)S(1)}, u32[]{:S(2)}, u32[]{:S(2)}) %collective-permute-start.4) | collective-permute-done | bytes 262176 | tf_op jit(solution)/shard_map/ppermute | solution.py:223
  123.9 0.0 collective-permute-done.5
  123.9 0.7 fusion
Async XLA Ops:
  1.8 93.7 %copy-start = (bf16[4,1,8,128,128]{4,3,2,1,0:T(8,128)(2,1)S(1)}, bf16[4,1,8,128,128]{4,3,2,1,0:T(8,128)(2,1)}, u32[]{:S(2)}) copy-start(bf16[4,1,8,128,128]{4,3,2,1,0:T(8,128)(2,1)} %param.4) | copy-start | bytes 3145732
  1.8 12.9 %all-to-all-start = ((bf16[4,288,128]{2,1,0:T(8,128)(2,1)}), bf16[4,288,128]{2,1,0:T(8,128)(2,1)S(1)}, u32[]{:S(2)}, u32[]{:S(2)}) async-start(bf16[4,288,128]{2,1,0:T(8,128)(2,1)} %shard_map.46), calls=%async_computation | async-start | bytes 589824 | tf_op jit(solution)/shard_map/all_to_all | solution.py:209
  6.2 89.3 %collective-permute-start.2 = (bf16[4,8,128,128]{3,2,1,0:T(8,128)(2,1)}, bf16[4,8,128,128]{3,2,1,0:T(8,128)(2,1)S(1)}, u32[]{:S(2)}, u32[]{:S(2)}) collective-permute-start(bf16[4,8,128,128]{3,2,1,0:T(8,128)(2,1)} %bitcast.10), channel_id=1, source_target_pairs={{0,12},{4,0},{8,4},{12,8},{1,13},{5,1},{9,5},{13,9},{2,14},{6,2},{... | collective-permute-start | bytes 3145736 | tf_op jit(solution)/shard_map/ppermute | solution.py:195
  8.4 87.2 %collective-permute-start.1 = (bf16[4,8,128,128]{3,2,1,0:T(8,128)(2,1)}, bf16[4,8,128,128]{3,2,1,0:T(8,128)(2,1)S(1)}, u32[]{:S(2)}, u32[]{:S(2)}) collective-permute-start(bf16[4,8,128,128]{3,2,1,0:T(8,128)(2,1)} %bitcast.11), channel_id=1, source_target_pairs={{0,8},{4,12},{8,0},{12,4},{1,9},{5,13},{9,1},{13,5},{2,10},{6,14},... | collective-permute-start | bytes 3145736 | tf_op jit(solution)/shard_map/ppermute | solution.py:195
  12.7 82.8 %collective-permute-start = (bf16[4,8,128,128]{3,2,1,0:T(8,128)(2,1)}, bf16[4,8,128,128]{3,2,1,0:T(8,128)(2,1)}, u32[]{:S(2)}, u32[]{:S(2)}) collective-permute-start(bf16[4,8,128,128]{3,2,1,0:T(8,128)(2,1)} %bitcast.12), channel_id=1, source_target_pairs={{0,4},{4,8},{8,12},{12,0},{1,5},{5,9},{9,13},{13,1},{2,6},{6,10},{... | collective-permute-start | bytes 3145736 | tf_op jit(solution)/shard_map/ppermute | solution.py:195
  106.6 14.6 %collective-permute-start.3 = (f32[4,128,128]{2,1,0:T(8,128)S(1)}, f32[4,128,128]{2,1,0:T(8,128)S(1)}, u32[]{:S(2)}, u32[]{:S(2)}) collective-permute-start(f32[4,128,128]{2,1,0:T(8,128)S(1)} %get-tuple-element.12), channel_id=1, source_target_pairs={{0,2},{1,3},{2,0},{3,1},{4,6},{5,7},{6,4},{7,5},{8,10},{9,11},{10,... | collective-permute-start | bytes 786440 | tf_op jit(solution)/shard_map/ppermute | solution.py:223
  108.5 15.4 %collective-permute-start.4 = (f32[4,128,128]{2,1,0:T(8,128)S(1)}, f32[4,128,128]{2,1,0:T(8,128)S(1)}, u32[]{:S(2)}, u32[]{:S(2)}) collective-permute-start(f32[4,128,128]{2,1,0:T(8,128)S(1)} %get-tuple-element.13), channel_id=1, source_target_pairs={{0,1},{1,2},{2,3},{3,0},{4,5},{5,6},{6,7},{7,4},{8,9},{9,10},{10,1... | collective-permute-start | bytes 786440 | tf_op jit(solution)/shard_map/ppermute | solution.py:223
  110.5 13.4 %collective-permute-start.5 = (f32[4,128,128]{2,1,0:T(8,128)S(1)}, f32[4,128,128]{2,1,0:T(8,128)S(1)}, u32[]{:S(2)}, u32[]{:S(2)}) collective-permute-start(f32[4,128,128]{2,1,0:T(8,128)S(1)} %get-tuple-element.14), channel_id=1, source_target_pairs={{0,3},{1,0},{2,1},{3,2},{4,7},{5,4},{6,5},{7,6},{8,11},{9,8},{10,9... | collective-permute-start | bytes 786440 | tf_op jit(solution)/shard_map/ppermute | solution.py:223

commit v7 on v6

--- a/solution.py
+++ b/solution.py
@@ -219,7 +219,7 @@
     gathered = lax.all_gather(code, ("z", "core"), axis=0)
     args = (place, small, factors, gathered)
     away = []
-    for t, part in zip((2, 1, 3), products((2, 1, 3), *args)):
+    for t, part in zip((3, 2, 1), products((3, 2, 1), *args)):
         away.append(lax.ppermute(part, "y", [(i, (i + t) % NY) for i in range(NY)]))
     total = products((0,), *args)[0] + away[0] + away[1] + away[2]
     return total.astype(jnp.bfloat16)[:, None]

time: 125 us -> 127 us (1.016)
  waiting for transfers between devices: 2.64 us -> 5.75 us
    ppermute x3, waiting for transfers between devices: 2.63 us -> 5.74 us  [per_device(): away.append(lax.ppermute(part, 'y', [(i, (i + t) % NY) for i in range(NY)]))]
where the time goes in v7:
time: 127 us
  blocking collectives  79.4 us (63%)
  Pallas kernels  20.5 us (16%)
  starting transfers between devices  20 us (16%)
  waiting for transfers between devices  5.75 us (5%)
    all_gather x1, blocking collectives, per_device(): gathered = lax.all_gather(code, ('z', 'core'), axis=0)  79.4 us
    pallas_call x2, Pallas kernels, products(): pl.pallas_call(functools.partial(product_kernel, turns), in_specs=[smem]...  17.3 us
    ppermute x3, starting transfers between devices, per_device(): lax.ppermute(factor, 'x', [(i, (i + s) % NX) for i in range(NX)])  8.41 us
    ppermute x3, starting transfers between devices, per_device(): away.append(lax.ppermute(part, 'y', [(i, (i + t) % NY) for i in range(NY)]))  7.2 us
    ppermute x3, waiting for transfers between devices, per_device(): away.append(lax.ppermute(part, 'y', [(i, (i + t) % NY) for i in range(NY)]))  5.74 us
    all_to_all x1, starting transfers between devices, per_device(): mine = lax.all_to_all(packed, 'x', 0, 0, tiled=True)  4.38 us
  transfers between devices with their start and end apart: 7, of which 1 were waited for; matrix products, arithmetic and copies ran while one was open for 0% of the time, Pallas kernels for 6%

profile of v7, /device:TPU:37, one launch (start us, length us, event | category | flops | bytes accessed | tf_op | source)
XLA Modules:
  0.0 126.5 jit_solution(17257895060138218069)
XLA Ops:
  0.0 1.8 %shard_map.46 = bf16[4,288,128]{2,1,0:T(8,128)(2,1)} custom-call(bf16[16,16,4,128]{3,2,1,0:T(4,128)(2,1)} %panel_hbm.1, s32[4,8]{1,0:T(4,128)} %bitcast.18, s32[32,16]{1,0:T(8,128)} %bitcast.17), custom_call_target="tpu_custom_call" | custom-call | tf_op jit(solution)/shard_map/pallas_call | solution.py:197
  1.8 0.0 copy-start
  1.8 4.4 %all-to-all-start = ((bf16[4,288,128]{2,1,0:T(8,128)(2,1)}), bf16[4,288,128]{2,1,0:T(8,128)(2,1)S(1)}, u32[]{:S(2)}, u32[]{:S(2)}) async-start(bf16[4,288,128]{2,1,0:T(8,128)(2,1)} %shard_map.46), calls=%async_computation | async-start | bytes 589824 | tf_op jit(solution)/shard_map/all_to_all | solution.py:209
  6.2 2.2 %collective-permute-start.2 = (bf16[4,8,128,128]{3,2,1,0:T(8,128)(2,1)}, bf16[4,8,128,128]{3,2,1,0:T(8,128)(2,1)S(1)}, u32[]{:S(2)}, u32[]{:S(2)}) collective-permute-start(bf16[4,8,128,128]{3,2,1,0:T(8,128)(2,1)} %bitcast.10), channel_id=1, source_target_pairs={{0,12},{4,0},{8,4},{12,8},{1,13},{5,1},{9,5},{13,9},{2,14},{6,2},{... | collective-permute-start | bytes 3145736 | tf_op jit(solution)/shard_map/ppermute | solution.py:195
  8.4 4.3 %collective-permute-start.1 = (bf16[4,8,128,128]{3,2,1,0:T(8,128)(2,1)}, bf16[4,8,128,128]{3,2,1,0:T(8,128)(2,1)S(1)}, u32[]{:S(2)}, u32[]{:S(2)}) collective-permute-start(bf16[4,8,128,128]{3,2,1,0:T(8,128)(2,1)} %bitcast.11), channel_id=1, source_target_pairs={{0,8},{4,12},{8,0},{12,4},{1,9},{5,13},{9,1},{13,5},{2,10},{6,14},... | collective-permute-start | bytes 3145736 | tf_op jit(solution)/shard_map/ppermute | solution.py:195
  12.7 1.9 %collective-permute-start = (bf16[4,8,128,128]{3,2,1,0:T(8,128)(2,1)}, bf16[4,8,128,128]{3,2,1,0:T(8,128)(2,1)}, u32[]{:S(2)}, u32[]{:S(2)}) collective-permute-start(bf16[4,8,128,128]{3,2,1,0:T(8,128)(2,1)} %bitcast.12), channel_id=1, source_target_pairs={{0,4},{4,8},{8,12},{12,0},{1,5},{5,9},{9,13},{13,1},{2,6},{6,10},{... | collective-permute-start | bytes 3145736 | tf_op jit(solution)/shard_map/ppermute | solution.py:195
  14.6 0.1 pad_add_fusion.place_ref
  14.7 0.0 all-to-all-done.shard_ref
  14.7 1.4 %shard_map.47 = (s16[1040,128]{1,0:T(8,128)(2,1)S(1)}, s32[128,128]{1,0:T(8,128)S(1)}) custom-call(bf16[4,288,128]{2,1,0:T(8,128)(2,1)S(1)} %all-to-all-done.shard_ref), custom_call_target="tpu_custom_call" | custom-call | tf_op jit(solution)/shard_map/pallas_call | solution.py:211
  16.1 79.4 %all-gather.2 = s16[33280,128]{1,0:T(8,128)(2,1)} all-gather(s16[1040,128]{1,0:T(8,128)(2,1)S(1)} %get-tuple-element.11), channel_id=2, replica_groups=mesh['z'=16,'core'=2,'x'=4,'y'=4] {'z','core'}, dimensions={0}, use_global_device_ids=true | all-gather | bytes 8785920 | tf_op jit(solution)/shard_map/all_gather | solution.py:219
  95.5 0.0 collective-permute-done.2.refs_3_
  95.5 0.0 collective-permute-done.1.refs_2_
  95.5 0.0 collective-permute-done.refs_1_
  95.5 0.0 copy-done
  95.5 11.1 %shard_map.49 = (f32[4,128,128]{2,1,0:T(8,128)S(1)}, f32[4,128,128]{2,1,0:T(8,128)S(1)}, f32[4,128,128]{2,1,0:T(8,128)S(1)}) custom-call(s32[2]{0:T(128)S(1)} %pad_add_fusion.place_ref, s32[128,128]{1,0:T(8,128)S(1)} %get-tuple-element.10.small_ref, bf16[4,8,128,128]{3,2,1,0:T(8,128)(2,1)S(1)} %bitcast.13, ...), custom_call_target="tpu_custom_call" | custom-call | flops 1610612736 | bytes 9437184 | tf_op jit(solution)/shard_map/pallas_call | solution.py:169
  106.6 1.9 %collective-permute-start.3 = (f32[4,128,128]{2,1,0:T(8,128)S(1)}, f32[4,128,128]{2,1,0:T(8,128)S(1)}, u32[]{:S(2)}, u32[]{:S(2)}) collective-permute-start(f32[4,128,128]{2,1,0:T(8,128)S(1)} %get-tuple-element.12), channel_id=1, source_target_pairs={{0,3},{1,0},{2,1},{3,2},{4,7},{5,4},{6,5},{7,6},{8,11},{9,8},{10,9... | collective-permute-start | bytes 786440 | tf_op jit(solution)/shard_map/ppermute | solution.py:223
  108.5 1.9 %collective-permute-start.4 = (f32[4,128,128]{2,1,0:T(8,128)S(1)}, f32[4,128,128]{2,1,0:T(8,128)S(1)}, u32[]{:S(2)}, u32[]{:S(2)}) collective-permute-start(f32[4,128,128]{2,1,0:T(8,128)S(1)} %get-tuple-element.13), channel_id=1, source_target_pairs={{0,2},{1,3},{2,0},{3,1},{4,6},{5,7},{6,4},{7,5},{8,10},{9,11},{10,... | collective-permute-start | bytes 786440 | tf_op jit(solution)/shard_map/ppermute | solution.py:223
  110.5 3.4 %collective-permute-start.5 = (f32[4,128,128]{2,1,0:T(8,128)S(1)}, f32[4,128,128]{2,1,0:T(8,128)S(1)}, u32[]{:S(2)}, u32[]{:S(2)}) collective-permute-start(f32[4,128,128]{2,1,0:T(8,128)S(1)} %get-tuple-element.14), channel_id=1, source_target_pairs={{0,1},{1,2},{2,3},{3,0},{4,5},{5,6},{6,7},{7,4},{8,9},{9,10},{10,1... | collective-permute-start | bytes 786440 | tf_op jit(solution)/shard_map/ppermute | solution.py:223
  113.8 6.2 %shard_map.48 = f32[4,128,128]{2,1,0:T(8,128)S(1)} custom-call(s32[2]{0:T(128)S(1)} %pad_add_fusion.place_ref, s32[128,128]{1,0:T(8,128)S(1)} %get-tuple-element.10.small_ref, bf16[4,8,128,128]{3,2,1,0:T(8,128)(2,1)S(1)} %bitcast.14, bf16[4,8,128,128]{3,2,1,0:T(8,128)(2,1)} %collective-permute-done.refs_1_, ...), custom_call_target="tpu_custom_call" | custom-call | flops 536870912 | bytes 3145728 | tf_op jit(solution)/shard_map/pallas_call | solution.py:169
  120.1 0.0 collective-permute-done.3
  120.1 0.0 collective-permute-done.4
  120.1 5.7 %collective-permute-done.5 = f32[4,128,128]{2,1,0:T(8,128)S(1)} collective-permute-done((f32[4,128,128]{2,1,0:T(8,128)S(1)}, f32[4,128,128]{2,1,0:T(8,128)S(1)}, u32[]{:S(2)}, u32[]{:S(2)}) %collective-permute-start.5) | collective-permute-done | bytes 262176 | tf_op jit(solution)/shard_map/ppermute | solution.py:223
  125.8 0.7 fusion
Async XLA Ops:
  1.8 93.7 %copy-start = (bf16[4,1,8,128,128]{4,3,2,1,0:T(8,128)(2,1)S(1)}, bf16[4,1,8,128,128]{4,3,2,1,0:T(8,128)(2,1)}, u32[]{:S(2)}) copy-start(bf16[4,1,8,128,128]{4,3,2,1,0:T(8,128)(2,1)} %param.4) | copy-start | bytes 3145732
  1.8 12.9 %all-to-all-start = ((bf16[4,288,128]{2,1,0:T(8,128)(2,1)}), bf16[4,288,128]{2,1,0:T(8,128)(2,1)S(1)}, u32[]{:S(2)}, u32[]{:S(2)}) async-start(bf16[4,288,128]{2,1,0:T(8,128)(2,1)} %shard_map.46), calls=%async_computation | async-start | bytes 589824 | tf_op jit(solution)/shard_map/all_to_all | solution.py:209
  6.2 89.3 %collective-permute-start.2 = (bf16[4,8,128,128]{3,2,1,0:T(8,128)(2,1)}, bf16[4,8,128,128]{3,2,1,0:T(8,128)(2,1)S(1)}, u32[]{:S(2)}, u32[]{:S(2)}) collective-permute-start(bf16[4,8,128,128]{3,2,1,0:T(8,128)(2,1)} %bitcast.10), channel_id=1, source_target_pairs={{0,12},{4,0},{8,4},{12,8},{1,13},{5,1},{9,5},{13,9},{2,14},{6,2},{... | collective-permute-start | bytes 3145736 | tf_op jit(solution)/shard_map/ppermute | solution.py:195
  8.4 87.2 %collective-permute-start.1 = (bf16[4,8,128,128]{3,2,1,0:T(8,128)(2,1)}, bf16[4,8,128,128]{3,2,1,0:T(8,128)(2,1)S(1)}, u32[]{:S(2)}, u32[]{:S(2)}) collective-permute-start(bf16[4,8,128,128]{3,2,1,0:T(8,128)(2,1)} %bitcast.11), channel_id=1, source_target_pairs={{0,8},{4,12},{8,0},{12,4},{1,9},{5,13},{9,1},{13,5},{2,10},{6,14},... | collective-permute-start | bytes 3145736 | tf_op jit(solution)/shard_map/ppermute | solution.py:195
  12.7 82.8 %collective-permute-start = (bf16[4,8,128,128]{3,2,1,0:T(8,128)(2,1)}, bf16[4,8,128,128]{3,2,1,0:T(8,128)(2,1)}, u32[]{:S(2)}, u32[]{:S(2)}) collective-permute-start(bf16[4,8,128,128]{3,2,1,0:T(8,128)(2,1)} %bitcast.12), channel_id=1, source_target_pairs={{0,4},{4,8},{8,12},{12,0},{1,5},{5,9},{9,13},{13,1},{2,6},{6,10},{... | collective-permute-start | bytes 3145736 | tf_op jit(solution)/shard_map/ppermute | solution.py:195
  106.6 13.4 %collective-permute-start.3 = (f32[4,128,128]{2,1,0:T(8,128)S(1)}, f32[4,128,128]{2,1,0:T(8,128)S(1)}, u32[]{:S(2)}, u32[]{:S(2)}) collective-permute-start(f32[4,128,128]{2,1,0:T(8,128)S(1)} %get-tuple-element.12), channel_id=1, source_target_pairs={{0,3},{1,0},{2,1},{3,2},{4,7},{5,4},{6,5},{7,6},{8,11},{9,8},{10,9... | collective-permute-start | bytes 786440 | tf_op jit(solution)/shard_map/ppermute | solution.py:223
  108.5 11.5 %collective-permute-start.4 = (f32[4,128,128]{2,1,0:T(8,128)S(1)}, f32[4,128,128]{2,1,0:T(8,128)S(1)}, u32[]{:S(2)}, u32[]{:S(2)}) collective-permute-start(f32[4,128,128]{2,1,0:T(8,128)S(1)} %get-tuple-element.13), channel_id=1, source_target_pairs={{0,2},{1,3},{2,0},{3,1},{4,6},{5,7},{6,4},{7,5},{8,10},{9,11},{10,... | collective-permute-start | bytes 786440 | tf_op jit(solution)/shard_map/ppermute | solution.py:223
  110.5 15.3 %collective-permute-start.5 = (f32[4,128,128]{2,1,0:T(8,128)S(1)}, f32[4,128,128]{2,1,0:T(8,128)S(1)}, u32[]{:S(2)}, u32[]{:S(2)}) collective-permute-start(f32[4,128,128]{2,1,0:T(8,128)S(1)} %get-tuple-element.14), channel_id=1, source_target_pairs={{0,1},{1,2},{2,3},{3,0},{4,5},{5,6},{6,7},{7,4},{8,9},{9,10},{10,1... | collective-permute-start | bytes 786440 | tf_op jit(solution)/shard_map/ppermute | solution.py:223
